TPU v7x, 32 devices: a whole 2x2x4 slice. The times are simulated.
32 devices in a mesh: series: 1, tm: 16 (over z, y, x), tile: 2 (over core).
Axes of the slice: x: 2, y: 2, z: 4, core: 2. Of those that a mesh axis runs over, the one named last changes fastest.
Arguments:
- frames: bfloat16 [128, 2304, 128], P('tm', ('series', 'tile')), may hold values from 0.001 to 6000, as said below
- block_cycle: int32 [2304], P('series'), may hold values from 0 to 31, as said below
- block_valid: int32 [2304], P('series'), may hold values from 1 to 128, as said below
- cycle_owner: int32 [32], replicated, may hold values from 0 to 31, each once
Outputs:
- two_time: float32 [4096, 128], P(('series', 'tm', 'tile'))
Inputs may be any that keep to these rules, and one draw needn't show every extreme that they name: `block_cycle`: each cycle is named by at least one block; in each aligned run of 1152 blocks no cycle is named by more than 71 blocks, and one cycle is named by exactly 71. The first block_valid[b] pixels of block b are valid. `frames`: positive intensities.
All inputs are finite; a program needn't handle non-finite values.
Results may differ from a plain program's by a relative error of at most 0.0003.
Values may be sent and summed in bfloat16 or wider, within the bound.
No kernel may reach another device: no remote copies, remote signals or barrier semaphores. Data moves between devices by JAX's collectives and lax.ppermute only.
A program may use at most 64 MiB of HBM per device.

v0:
```python
import jax
import jax.numpy as jnp
from jax import lax
from jax.sharding import PartitionSpec as P


def normalize(pixel_intensity, valid_count, lanes):
    lane_index = jnp.arange(lanes, dtype=jnp.int32)
    valid_mask = lane_index[None, :] < valid_count[:, None]
    pixel_mean = jnp.sum(pixel_intensity, axis=0) / pixel_intensity.shape[0]
    guarded_average = jnp.where(valid_mask, pixel_mean, jnp.float32(1.0))
    return jnp.where(valid_mask[None], pixel_intensity / guarded_average[None], jnp.float32(0.0))


def on_device(frames, block_cycle, block_valid, cycle_owner):
    tm_count = lax.axis_size("tm")
    tile_count = lax.axis_size("tile")
    tm_index = lax.axis_index("tm")
    tile_index = lax.axis_index("tile")
    local_frames = frames.shape[0]
    half = frames.shape[1]
    lanes = frames.shape[2]
    cycle_count = cycle_owner.shape[0]
    frame_count = local_frames * tm_count
    cycle_range = jnp.arange(cycle_count, dtype=jnp.int32)
    member_all = (block_cycle[None, :] == cycle_owner[:, None]).astype(jnp.float32)
    pixel_total = jnp.dot(
        member_all, block_valid.astype(jnp.float32), precision=lax.Precision.HIGHEST
    )
    row_count = cycle_count * frame_count // (tm_count * tile_count)
    block_local = half // tm_count
    reshaped = frames.reshape(local_frames, tm_count, block_local, lanes)
    arrived = lax.all_to_all(reshaped, "tm", split_axis=1, concat_axis=0, tiled=True)
    pixel_intensity = arrived.reshape(frame_count, block_local, lanes).astype(jnp.float32)
    offset = (tile_index * tm_count + tm_index) * block_local
    cycle_ids = lax.dynamic_slice_in_dim(block_cycle, offset, block_local, 0)
    valid_count = lax.dynamic_slice_in_dim(block_valid, offset, block_local, 0)
    members = (cycle_ids[None, :] == cycle_owner[:, None]).astype(jnp.float32)
    normalized_frames = normalize(pixel_intensity, valid_count, lanes)
    gram_matrices = jnp.einsum(
        "rnk,jnk->nrj", normalized_frames, normalized_frames, precision=lax.Precision.HIGHEST
    )
    partial_value = jnp.dot(
        members,
        gram_matrices.reshape(block_local, frame_count * frame_count),
        precision=lax.Precision.HIGHEST,
    )
    partial_value = partial_value.reshape(cycle_count * frame_count, frame_count)
    frame_sums = jnp.dot(
        members, jnp.sum(normalized_frames, axis=2).T, precision=lax.Precision.HIGHEST
    )
    owned = lax.psum_scatter(partial_value, ("tm", "tile"), scatter_dimension=0, tiled=True)
    frame_total = lax.psum(frame_sums, ("tm", "tile"))
    row_start = (tm_index * tile_count + tile_index) * row_count
    row_global = row_start + jnp.arange(row_count, dtype=jnp.int32)
    slot_index = row_global // frame_count
    frame_time_index = row_global % frame_count
    select = (slot_index[:, None] == cycle_range[None, :]).astype(jnp.float32)
    row_sums = jnp.dot(select, frame_total, precision=lax.Precision.HIGHEST)
    row_pixels = jnp.dot(select, pixel_total, precision=lax.Precision.HIGHEST)
    time_pick = (
        jnp.arange(frame_count, dtype=jnp.int32)[None, :] == frame_time_index[:, None]
    ).astype(jnp.float32)
    first_sums = jnp.sum(row_sums * time_pick, axis=1)
    return row_pixels[:, None] * owned / (first_sums[:, None] * row_sums)


def solution(mesh):
    in_specs = (P("tm", ("series", "tile"), None), P("series"), P("series"), P())
    out_specs = P(("series", "tm", "tile"), None)
    return jax.shard_map(
        on_device, mesh=mesh, in_specs=in_specs, out_specs=out_specs, check_vma=False
    )
```

profile of v0, /device:TPU:0, one launch (start us, length us, event | category | flops | bytes accessed | tf_op | source)
XLA Modules:
  0.0 240.3 jit_solution(12396194771923086887)
XLA Ops:
  6.5 0.0 copy-start.2
  6.5 0.0 copy-start
  6.5 3.4 %copy.12 = bf16[8,16,72,128]{3,2,0,1:T(8,128)(2,1)} copy(bf16[8,16,72,128]{3,2,1,0:T(8,128)(2,1)} %bitcast.32) | data formatting | bytes 4718592 | tf_op jit(solution)/shard_map/reshape | solution.py:32
  10.0 8.3 %all-to-all-start = ((bf16[8,16,72,128]{3,2,0,1:T(8,128)(2,1)}), bf16[8,16,72,128]{3,2,0,1:T(8,128)(2,1)S(1)}, u32[]{:S(2)}, u32[]{:S(2)}) async-start(bf16[8,16,72,128]{3,2,0,1:T(8,128)(2,1)} %copy.12), calls=%async_computation | async-start | bytes 4718592 | tf_op jit(solution)/shard_map/all_to_all | solution.py:33
  18.3 0.0 reduce-scatter.2.cloned.1.call-start
  18.4 0.0 copy-done.2
  18.4 0.1 dynamic_slice.6
  18.5 0.0 copy-done
  18.5 0.1 dynamic_slice.7
  18.5 0.1 iota_compare_fusion.4
  18.6 47.3 %all-to-all-done = bf16[8,16,72,128]{3,2,0,1:T(8,128)(2,1)S(1)} async-done(((bf16[8,16,72,128]{3,2,0,1:T(8,128)(2,1)}), bf16[8,16,72,128]{3,2,0,1:T(8,128)(2,1)S(1)}, u32[]{:S(2)}, u32[]{:S(2)}) %all-to-all-start) | async-done | bytes 2359328 | tf_op jit(solution)/shard_map/all_to_all | solution.py:33
  65.9 0.4 bitcast_reduce_fusion
  66.3 0.1 multiply_select_fusion
  66.4 0.5 bitcast_convert_fusion
  66.9 0.0 copy-start.1
  66.9 10.8 %fusion.5 = f32[72,128,128]{2,1,0:T(8,128)S(1)} fusion(f32[128,72,128]{2,1,0:T(8,128)S(1)} %bitcast.31, f32[72,128]{1,0:T(8,128)S(1)} %multiply_select_fusion, pred[72,128]{1,0:T(8,128)(4,1)S(1)} %iota_compare_fusion.4), kind=kOutput, calls=%fused_computation.8 | convolution fusion | flops 1814298624 | bytes 9483264 | tf_op jit(solution)/shard_map/rnk,jnk->nrj/dot_general | solution.py:40
  77.7 0.0 copy-done.1
  77.7 6.1 %fusion = f32[32,16384]{1,0:T(8,128)} fusion(f32[9,8,128,128]{3,2,1,0:T(8,128)S(1)} %bitcast.30, s32[72]{0:T(128)S(1)} %dynamic_slice.6, s32[32]{0:T(128)S(1)} %copy-done.1), kind=kOutput, calls=%fused_computation | convolution fusion | flops 452987136 | bytes 6816160 | tf_op jit(solution)/shard_map/dot_general | solution.py:43
  83.8 2.7 %reshape.93 = f32[4096,128]{1,0:T(8,128)} reshape(f32[32,16384]{1,0:T(8,128)} %fusion) | data formatting | bytes 4194304 | tf_op jit(solution)/shard_map/reshape | solution.py:48
  86.5 2.9 %copy.14 = f32[4096,128]{0,1:T(8,128)} copy(f32[4096,128]{1,0:T(8,128)} %reshape.93) | data formatting | bytes 4194304 | tf_op jit(solution)/shard_map/reshape | solution.py:48
  89.4 0.0 reduce-scatter.2.cloned.1.call-update
  89.5 0.3 convolution_bitcast_fusion
  89.8 0.2 convolution_bitcast_fusion.1
  90.0 2.3 fusion.7
  92.3 0.2 fusion.14
  92.5 46.6 %psum.7 = f32[32,128]{1,0:T(8,128)S(1)} all-reduce(f32[32,128]{1,0:T(8,128)S(1)} %fusion.14), channel_id=1, replica_groups=mesh['series'=1,'tm'=16,'tile'=2] {'tm','tile'}, use_global_device_ids=true, to_apply=%region_3.4 | all-reduce | flops 4096 | bytes 32768 | tf_op jit(solution)/shard_map/psum | solution.py:53
  139.1 0.3 select_reduce_fusion
  139.4 92.5 %reduce-scatter.2.cloned.1.call-done = f32[128,128]{0,1:T(8,128)} async-done(((f32[4096,128]{0,1:T(8,128)}), f32[128,128]{0,1:T(8,128)}) %reduce-scatter.2.cloned.1.call-update) | async-done | bytes 65552 | tf_op jit(solution)/shard_map/reduce_scatter | solution.py:52
  231.9 0.9 multiply_divide_fusion
  232.7 0.7 copy.17
  (4 shorter events, 0.0 us)
Async XLA Ops:
  6.5 11.8 %copy-start.2 = (s32[2304]{0:T(1024)S(1)}, s32[2304]{0:T(1024)}, u32[]{:S(2)}) copy-start(s32[2304]{0:T(1024)} %param.5) | copy-start | bytes 27652
  6.5 11.9 %copy-start = (s32[2304]{0:T(1024)S(1)}, s32[2304]{0:T(1024)}, u32[]{:S(2)}) copy-start(s32[2304]{0:T(1024)} %param.6) | copy-start | bytes 27652
  10.0 55.9 %all-to-all-start = ((bf16[8,16,72,128]{3,2,0,1:T(8,128)(2,1)}), bf16[8,16,72,128]{3,2,0,1:T(8,128)(2,1)S(1)}, u32[]{:S(2)}, u32[]{:S(2)}) async-start(bf16[8,16,72,128]{3,2,0,1:T(8,128)(2,1)} %copy.12), calls=%async_computation | async-start | bytes 4718592 | tf_op jit(solution)/shard_map/all_to_all | solution.py:33
  18.3 213.6 %reduce-scatter.2.cloned.1.call-start = ((), (), s32[]{:S(2)}) async-start(), calls=%async_computation.2 | async-start | bytes 2162688 | tf_op jit(solution)/shard_map/reduce_scatter | solution.py:52
  66.9 10.8 %copy-start.1 = (s32[32]{0:T(128)S(1)}, s32[32]{0:T(128)}, u32[]{:S(2)}) copy-start(s32[32]{0:T(128)} %param.7) | copy-start | bytes 388
Sparse Core Ops, SparseCore 0:
  89.5 142.2 reduce-scatter.1
where the time goes:
time: 241 us; the launch traced here: 240 us
  waiting for transfers between devices  140 us (58%)
  blocking collectives  46.6 us (19%)
  matrix products  17.9 us (7%)
  between operations  13.5 us (6%)
  local copies, waits for them, and re-layouts  9.96 us (4%)
  starting transfers between devices  8.35 us (3%)
  other arithmetic  4.21 us (2%)
    reduce_scatter x1, waiting for transfers between devices, on_device(): lax.psum_scatter(partial_value, ('tm', 'tile'), scatter_dimension=0, tile...  92.5 us
    all_to_all x1, waiting for transfers between devices, on_device(): lax.all_to_all(reshaped, 'tm', split_axis=1, concat_axis=0, tiled=True)  47.3 us
    psum x1, blocking collectives, on_device(): frame_total = lax.psum(frame_sums, ('tm', 'tile'))  46.6 us
    dot_general x1, matrix products, on_device(): jnp.einsum('rnk,jnk->nrj', normalized_frames, normalized_frames, precisio...  10.8 us
    all_to_all x1, starting transfers between devices, on_device(): lax.all_to_all(reshaped, 'tm', split_axis=1, concat_axis=0, tiled=True)  8.31 us
    dot_general x1, matrix products, on_device(): jnp.dot(members, gram_matrices.reshape(block_local, frame_count * frame_c...  6.09 us
    reshape x2, local copies, waits for them, and re-layouts, on_device(): partial_value.reshape(cycle_count * frame_count, frame_count)  5.61 us
  transfers between devices with their start and end apart: 2, of which 2 were waited for; matrix products, arithmetic and copies ran while one was open for 1% of the time, Pallas kernels for 0%

commit v1 on v0

--- a/solution.py
+++ b/solution.py
@@ -1,7 +1,240 @@
+import functools
+
 import jax
 import jax.numpy as jnp
 from jax import lax
+from jax.experimental import pallas as pl
+from jax.experimental.pallas import tpu as pltpu
 from jax.sharding import PartitionSpec as P
+
+LANE = 128
+UNROLL = 8
+VMEM_LIMIT = 48 * 1024 * 1024
+LADDER = (16, 24, 32, 36, 40, 42, 44, 46, 48, 52, 56, 64, 80, 104, 144)
+NT = (((1,), (1,)), ((), ()))
+
+
+def plan_kernel(where_ref, cycle_ref, valid_ref, owner_ref, block_ref, start_ref, scalar_ref):
+    tm_index, tile_index = where_ref[0], where_ref[1]
+    block_count = cycle_ref.shape[1]
+    chunks = block_count // LANE
+    slots = owner_ref.shape[0]
+    list_rows = block_ref.shape[0]
+    owner = owner_ref[...]
+    slot = lax.broadcasted_iota(jnp.int32, (slots, LANE), 0)
+    mine = (slot % 2 == tile_index).astype(jnp.float32)
+
+    member, weighted = [], []
+    for k in range(chunks):
+        cut = slice(k * LANE, (k + 1) * LANE)
+        hit = (cycle_ref[:, cut] == owner).astype(jnp.float32)
+        member.append(hit)
+        weighted.append(hit * valid_ref[:, cut].astype(jnp.float32))
+    stacked = jnp.concatenate(member + weighted, axis=0).astype(jnp.bfloat16)
+    before = lax.broadcasted_iota(jnp.int32, (LANE, 2 * LANE), 0)
+    column = lax.broadcasted_iota(jnp.int32, (LANE, 2 * LANE), 1)
+    prefix = ((before < column) | (column >= LANE)).astype(jnp.float32).astype(jnp.bfloat16)
+    sums = jnp.dot(stacked, prefix, preferred_element_type=jnp.float32)
+
+    count = jnp.zeros((slots, LANE), jnp.float32)
+    pixels = jnp.zeros((slots, LANE), jnp.float32)
+    rank, start = [], []
+    for k in range(chunks):
+        low = slice(k * slots, (k + 1) * slots)
+        high = slice((chunks + k) * slots, (chunks + k + 1) * slots)
+        rank.append(count + sums[low, :LANE])
+        start.append(jnp.sum(member[k] * (pixels + sums[high, :LANE]), axis=0, keepdims=True))
+        count = count + sums[low, LANE:]
+        pixels = pixels + sums[high, LANE:]
+
+    row = lax.broadcasted_iota(jnp.int32, (slots, slots), 0)
+    col = lax.broadcasted_iota(jnp.int32, (slots, slots), 1)
+    earlier = ((col < row) & (col % 2 == tile_index)).astype(jnp.float32)
+    base = jnp.dot(
+        earlier, count, precision=lax.Precision.HIGHEST, preferred_element_type=jnp.float32
+    )
+
+    list_row = lax.broadcasted_iota(jnp.int32, (list_rows, LANE), 0)
+    list_col = lax.broadcasted_iota(jnp.int32, (LANE, LANE), 0)
+    lane = lax.broadcasted_iota(jnp.int32, (1, LANE), 1)
+    half_slot = (slot // 2).astype(jnp.float32)
+    lists = jnp.zeros((4 * list_rows, LANE), jnp.float32)
+    for k in range(chunks):
+        own = member[k] * mine
+        place = jnp.sum(own * (rank[k] + base), axis=0, keepdims=True).astype(jnp.int32)
+        target = jnp.sum(own * half_slot, axis=0, keepdims=True).astype(jnp.int32)
+        used = jnp.sum(own, axis=0, keepdims=True) > 0
+        begin = start[k].astype(jnp.int32)
+        block = k * LANE + lane
+        at_row = list_row == jnp.where(used, place // LANE, -1)
+        at_col = (list_col == place % LANE).astype(jnp.float32).astype(jnp.bfloat16)
+        parts = (block % 256, block // 256 + 16 * target, begin % 256, begin // 256)
+        spread = jnp.concatenate(
+            [jnp.where(at_row, part.astype(jnp.float32), 0.0) for part in parts], axis=0
+        ).astype(jnp.bfloat16)
+        lists = lists + lax.dot_general(spread, at_col, NT, preferred_element_type=jnp.float32)
+    lists = lists.astype(jnp.int32)
+    block_ref[...] = lists[:list_rows] + 256 * lists[list_rows : 2 * list_rows]
+    start_ref[...] = lists[2 * list_rows : 3 * list_rows] + 256 * lists[3 * list_rows :]
+
+    most = jnp.max(pixels).astype(jnp.int32)
+    rows = (most + LANE - 1) // LANE
+    rung = jnp.int32(0)
+    for size in LADDER[:-1]:
+        rung = rung + (rows > size).astype(jnp.int32)
+    own_slot = 2 * tm_index + tile_index
+    scalar_ref[0] = rung
+    scalar_ref[1] = jnp.sum(count[:, :1] * mine[:, :1]).astype(jnp.int32)
+    scalar_ref[2] = jnp.sum(jnp.where(slot == own_slot, pixels, 0.0)[:, :1]).astype(jnp.int32)
+    scalar_ref[3] = tile_index
+
+
+def pack_kernel(size, block_ref, start_ref, scalar_ref, near_ref, far_ref, out_ref, pool, stage):
+    frames, half, _ = near_ref.shape
+    near_at = scalar_ref[3] * half
+    far_at = half - near_at
+    step = 64
+    for source, at in ((near_ref, near_at), (far_ref, far_at)):
+        for f in range(frames):
+
+            def widen(i, _, source=source, at=at, f=f):
+                begin = pl.multiple_of(i * step, step)
+                to = pl.multiple_of(f * 2 * half + at + begin, 8)
+                pool[pl.ds(to, step), :] = source[f, pl.ds(begin, step), :].astype(jnp.float32)
+                return 0
+
+            lax.fori_loop(0, half // step, widen, 0)
+
+    lane = lax.broadcasted_iota(jnp.int32, (frames, LANE), 1)
+
+    def place(i, carry):
+        held, spill, last = carry
+        word = block_ref[i]
+        begin = start_ref[i]
+        block = word & 4095
+        row = (word >> 12) * size + (begin >> 7)
+        shift = begin & (LANE - 1)
+        x = pool[pl.ds(block, frames, stride=2 * half), :]
+        turned = pltpu.roll(x, shift, 1)
+        held = jnp.where(lane >= shift, turned, jnp.where(row == last, held, spill))
+        at = pl.multiple_of(row * frames, frames)
+        stage[pl.ds(at, frames), :] = held
+        stage[pl.ds(at + frames, frames), :] = turned
+        return held, turned, row
+
+    def group(j, carry):
+        for i in range(UNROLL):
+            carry = place(j * UNROLL + i, carry)
+        return carry
+
+    total = scalar_ref[1]
+    zero = jnp.zeros((frames, LANE), jnp.float32)
+    carry = lax.fori_loop(0, total // UNROLL, group, (zero, zero, jnp.int32(-1)))
+    lax.fori_loop(total // UNROLL * UNROLL, total, place, carry)
+
+    depth = size * frames
+    for d in range(out_ref.shape[0]):
+        out_ref[d] = stage[d * depth : (d + 1) * depth, :].astype(jnp.bfloat16)
+
+
+def gram_kernel(scalar_ref, x_ref, out_ref):
+    sources = x_ref.shape[0]
+    frames = out_ref.shape[0]
+    local = frames // sources
+    pixels = scalar_ref[2]
+    lane = lax.broadcasted_iota(jnp.int32, (1, LANE), 1)
+
+    def pair(j, carry):
+        gram, total = carry
+        both = x_ref[:, pl.ds(pl.multiple_of(j * 2 * local, 2 * local), 2 * local), :]
+        both = both.astype(jnp.float32).reshape(sources, 2, local, LANE)
+        exact, high, low = [], [], []
+        for i in range(2):
+            used = lane + (2 * j + i) * LANE < pixels
+            x = jnp.where(used, both[:, i].reshape(frames, LANE), 0.0)
+            mean = jnp.where(used, jnp.sum(x, axis=0, keepdims=True) / frames, 1.0)
+            scale = 1.0 / mean
+            total = total + x * scale
+            y = x * (scale * scale)
+            top = y.astype(jnp.bfloat16)
+            exact.append(x.astype(jnp.bfloat16))
+            high.append(top)
+            low.append((y - top.astype(jnp.float32)).astype(jnp.bfloat16))
+        left = jnp.concatenate(exact, axis=1)
+        right = jnp.concatenate(
+            [jnp.concatenate(high, axis=1), jnp.concatenate(low, axis=1)], axis=0
+        )
+        gram = gram + lax.dot_general(left, right, NT, preferred_element_type=jnp.float32)
+        return gram, total
+
+    start = (jnp.zeros((frames, 2 * frames), jnp.float32), jnp.zeros((frames, LANE), jnp.float32))
+    gram, total = lax.fori_loop(0, (pixels + 2 * LANE - 1) // (2 * LANE), pair, start)
+    gram = gram[:, :frames] + gram[:, frames:]
+    first = jnp.sum(total, axis=1, keepdims=True)
+    second = jnp.sum(total.T, axis=0, keepdims=True)
+    out_ref[...] = pixels.astype(jnp.float32) * gram / (first * second)
+
+
+def on_device_routed(frames, block_cycle, block_valid, cycle_owner):
+    tm_count = lax.axis_size("tm")
+    local_frames, half, _ = frames.shape
+    block_count = block_cycle.shape[0]
+    slots = cycle_owner.shape[0]
+    list_rows = -(-block_count // (8 * LANE)) * 8
+    vmem = pl.BlockSpec(memory_space=pltpu.VMEM)
+    smem = pl.BlockSpec(memory_space=pltpu.SMEM)
+    params = pltpu.CompilerParams(vmem_limit_bytes=VMEM_LIMIT)
+
+    far = lax.ppermute(frames, "tile", [(0, 1), (1, 0)])
+    where = jnp.stack([lax.axis_index("tm"), lax.axis_index("tile")]).astype(jnp.int32)
+    block_list, start_list, scalars = pl.pallas_call(
+        plan_kernel,
+        out_shape=(
+            jax.ShapeDtypeStruct((list_rows, LANE), jnp.int32),
+            jax.ShapeDtypeStruct((list_rows, LANE), jnp.int32),
+            jax.ShapeDtypeStruct((4,), jnp.int32),
+        ),
+        in_specs=[smem, vmem, vmem, vmem],
+        out_specs=(vmem, vmem, smem),
+        compiler_params=params,
+        name="plan",
+    )(where, block_cycle[None, :], block_valid[None, :], cycle_owner[:, None])
+    block_list = block_list.reshape(-1)
+    start_list = start_list.reshape(-1)
+
+    def branch(size):
+        def run(block_list, start_list, scalars, near, far):
+            send = pl.pallas_call(
+                functools.partial(pack_kernel, size),
+                out_shape=jax.ShapeDtypeStruct(
+                    (tm_count, size * local_frames, LANE), jnp.bfloat16
+                ),
+                in_specs=[smem, smem, smem, vmem, vmem],
+                out_specs=vmem,
+                scratch_shapes=[
+                    pltpu.VMEM((local_frames * 2 * half, LANE), jnp.float32),
+                    pltpu.VMEM(((tm_count * size + 1) * local_frames, LANE), jnp.float32),
+                ],
+                compiler_params=params,
+                name="pack",
+            )(block_list, start_list, scalars, near, far)
+            got = lax.all_to_all(send, "tm", split_axis=0, concat_axis=0, tiled=True)
+            return pl.pallas_call(
+                gram_kernel,
+                out_shape=jax.ShapeDtypeStruct(
+                    (tm_count * local_frames, tm_count * local_frames), jnp.float32
+                ),
+                in_specs=[smem, vmem],
+                out_specs=vmem,
+                compiler_params=params,
+                name="gram",
+            )(scalars, got)
+
+        return run
+
+    return lax.switch(
+        scalars[0], [branch(size) for size in LADDER], block_list, start_list, scalars, frames, far
+    )
 
 
 def normalize(pixel_intensity, valid_count, lanes):
@@ -12,7 +245,7 @@
     return jnp.where(valid_mask[None], pixel_intensity / guarded_average[None], jnp.float32(0.0))
 
 
-def on_device(frames, block_cycle, block_valid, cycle_owner):
+def on_device_summed(frames, block_cycle, block_valid, cycle_owner):
     tm_count = lax.axis_size("tm")
     tile_count = lax.axis_size("tile")
     tm_index = lax.axis_index("tm")
@@ -68,6 +301,18 @@
 def solution(mesh):
     in_specs = (P("tm", ("series", "tile"), None), P("series"), P("series"), P())
     out_specs = P(("series", "tm", "tile"), None)
+
+    def on_device(frames, block_cycle, block_valid, cycle_owner):
+        routed = (
+            mesh.shape["tile"] == 2
+            and mesh.shape["tm"] * 2 == cycle_owner.shape[0]
+            and frames.shape[0] == 8
+            and mesh.shape["tm"] * 8 == LANE
+            and block_cycle.shape[0] <= 4096
+        )
+        body = on_device_routed if routed else on_device_summed
+        return body(frames, block_cycle, block_valid, cycle_owner)
+
     return jax.shard_map(
         on_device, mesh=mesh, in_specs=in_specs, out_specs=out_specs, check_vma=False
     )

time: 241 us -> 72.2 us (0.30)
  waiting for transfers between devices: 140 us -> 0.26 us
  Pallas kernels: 0 us -> 26.1 us
  matrix products: 17.9 us -> 0 us
  between operations: 13.5 us -> 0.06 us
  starting transfers between devices: 8.35 us -> 0.45 us
  local copies, waits for them, and re-layouts: 9.96 us -> 2.79 us
  blocking collectives: 46.6 us -> 42.1 us
  other arithmetic: 4.21 us -> 0.07 us
    reduce_scatter x1 -> x0, waiting for transfers between devices: 92.5 us -> none  [on_device(): lax.psum_scatter(partial_value, ('tm', 'tile'), scatter_dimension=0, tile...]
    all_to_all x1 -> x0, waiting for transfers between devices: 47.3 us -> none  [on_device(): lax.all_to_all(reshaped, 'tm', split_axis=1, concat_axis=0, tiled=True)]
    psum x1 -> x0, blocking collectives: 46.6 us -> none  [on_device(): frame_total = lax.psum(frame_sums, ('tm', 'tile'))]
    all_to_all x0 -> x1, blocking collectives: none -> 42.1 us  [run(): got = lax.all_to_all(send, 'tm', split_axis=0, concat_axis=0, tiled=True)]
    pallas_call x0 -> x3, Pallas kernels: none -> 26.1 us  [the longest x1 18.9 us: run(): pl.pallas_call(functools.partial(pack_kernel, size), out_shape=jax.ShapeD...]
    dot_general x6 -> x0, matrix products: 17.9 us -> none  [the longest x1 10.8 us: on_device(): jnp.einsum('rnk,jnk->nrj', normalized_frames, normalized_frames, precisio...]
    reshape x3 -> x0, local copies, waits for them, and re-layouts: 9.05 us -> none  [the longest x2 5.61 us: on_device(): partial_value.reshape(cycle_count * frame_count, frame_count)]
    all_to_all x1 -> x0, starting transfers between devices: 8.31 us -> none  [on_device(): lax.all_to_all(reshaped, 'tm', split_axis=1, concat_axis=0, tiled=True)]
  transfers between devices with their start and end apart: 2 -> 1, of which waited for: 2 -> 1; matrix products, arithmetic and copies ran while one was open for 1% -> 3% of each run, Pallas kernels for 0% -> 3%
where the time goes in v1:
time: 72.2 us; the launch traced here: 71.9 us
  blocking collectives  42.1 us (58%)
  Pallas kernels  26.1 us (36%)
  local copies, waits for them, and re-layouts  2.79 us (4%)
    all_to_all x1, blocking collectives, run(): got = lax.all_to_all(send, 'tm', split_axis=0, concat_axis=0, tiled=True)  42.1 us
    pallas_call x1, Pallas kernels, run(): pl.pallas_call(functools.partial(pack_kernel, size), out_shape=jax.ShapeD...  18.9 us
    pallas_call x1, Pallas kernels, run(): pl.pallas_call(gram_kernel, out_shape=jax.ShapeDtypeStruct((tm_count * lo...  5.3 us
    pallas_call x1, Pallas kernels, on_device_routed(): pl.pallas_call(plan_kernel, out_shape=(jax.ShapeDtypeStruct((list_rows, L...  1.83 us
  transfers between devices with their start and end apart: 1, of which 1 were waited for; matrix products, arithmetic and copies ran while one was open for 3% of the time, Pallas kernels for 3%

profile of v1, /device:TPU:0, one launch (start us, length us, event | category | flops | bytes accessed | tf_op | source)
XLA Modules:
  0.0 71.9 jit_solution(2443625901183943106)
XLA Ops:
  0.0 0.5 collective-permute-start
  0.5 0.7 broadcast_in_dim.9.cycle_ref
  1.2 0.7 broadcast_in_dim.10.valid_ref
  1.9 0.7 %copy.20.owner_ref = s32[32,1]{1,0:T(8,128)S(1)} copy(s32[32,1]{0,1:T(1,128)} %bitcast.66) | data formatting | bytes 256 | tf_op jit(solution)/shard_map/broadcast_in_dim | solution.py:201
  2.6 0.1 pad_add_fusion.where_ref
  2.7 1.8 %plan.1 = (s32[24,128]{1,0:T(8,128)S(1)}, s32[24,128]{1,0:T(8,128)S(1)}, s32[4]{0:T(128)S(1)}) custom-call(s32[2]{0:T(128)S(1)} %pad_add_fusion.where_ref, s32[1,2304]{1,0:T(1,128)S(1)} %broadcast_in_dim.9.cycle_ref, s32[1,2304]{1,0:T(1,128)S(1)} %broadcast_in_dim.10.valid_ref, s32[32,1]{1,0:T(8,128)S(1)} %copy.20.owner_ref), custom_call_target="tpu_custom_call" | custom-call | tf_op jit(solution)/shard_map/plan/pallas_call | solution.py:190
  4.6 0.3 collective-permute-done
  4.8 66.4 %conditional.1 = (f32[128,128]{1,0:T(8,128)S(1)}) conditional(s32[]{:T(128)} %bitcast.33, (s32[24,128]{1,0:T(8,128)S(1)}, s32[24,128]{1,0:T(8,128)S(1)}, s32[4]{0:T(128)S(1)}, bf16[8,1152,128]{2,1,0:T(8,128)(2,1)}, bf16[8,1152,128]{2,1,0:T(8,128)(2,1)S(1)}) %tuple.50, (s32[24,128]{1,0:T(8,128)S(1)}, ...), branch_computations={%region_0.0_spmd, %region_1.0_spmd, %region_2.0_spmd, %region_3.0_... | conditional | bytes 9437192 | solution.py:235
  4.8 18.9 %pack.20 = bf16[16,336,128]{2,1,0:T(8,128)(2,1)S(1)} custom-call(s32[3072]{0:T(1024)S(1)} %bitcast.40, s32[3072]{0:T(1024)S(1)} %bitcast.55, s32[4]{0:T(128)S(1)} %get-tuple-element.196.scalar_ref, bf16[8,1152,128]{2,1,0:T(8,128)(2,1)} %get-tuple-element.199.near_ref, bf16[8,1152,128]{2,1,0:T(8,128)(2,1)S(1)} %get-tuple-element.200.far_ref), custom_call_target="tpu_custom_call" | custom-call | tf_op jit(solution)/shard_map/cond/branch_5_fun/pack/pallas_call | solution.py:207
  23.8 42.1 %all_to_all.65.x_ref = bf16[16,336,128]{2,1,0:T(8,128)(2,1)S(1)} all-to-all(bf16[16,336,128]{2,1,0:T(8,128)(2,1)S(1)} %pack.20), channel_id=1, replica_groups=mesh['series'=1,'tm'=16,'tile'=2] {'tm'}, dimensions={0} | all-to-all | bytes 2752512 | tf_op jit(solution)/shard_map/cond/branch_5_fun/all_to_all | solution.py:221
  65.9 5.3 %gram.20 = f32[128,128]{1,0:T(8,128)S(1)} custom-call(s32[4]{0:T(128)S(1)} %get-tuple-element.196.scalar_ref, bf16[16,336,128]{2,1,0:T(8,128)(2,1)S(1)} %all_to_all.65.x_ref), custom_call_target="tpu_custom_call" | custom-call | tf_op jit(solution)/shard_map/cond/branch_5_fun/gram/pallas_call | solution.py:222
  71.2 0.0 copy-start
  71.2 0.6 copy-done
Async XLA Ops:
  0.0 4.8 %collective-permute-start = (bf16[8,1152,128]{2,1,0:T(8,128)(2,1)}, bf16[8,1152,128]{2,1,0:T(8,128)(2,1)S(1)}, u32[]{:S(2)}, u32[]{:S(2)}) collective-permute-start(bf16[8,1152,128]{2,1,0:T(8,128)(2,1)} %param.19), channel_id=1, source_target_pairs={{0,1},{1,0},{2,3},{3,2},{4,5},{5,4},{6,7},{7,6},{8,9},{9,8},{10,11... | collective-permute-start | bytes 7077896 | tf_op jit(solution)/shard_map/ppermute | solution.py:188
  71.2 0.6 copy-start

commit v2 on v1

--- a/solution.py
+++ b/solution.py
@@ -9,27 +9,29 @@
 
 LANE = 128
 UNROLL = 8
+STEP = 192
 VMEM_LIMIT = 48 * 1024 * 1024
 LADDER = (16, 24, 32, 36, 40, 42, 44, 46, 48, 52, 56, 64, 80, 104, 144)
 NT = (((1,), (1,)), ((), ()))
 
 
-def plan_kernel(where_ref, cycle_ref, valid_ref, owner_ref, block_ref, start_ref, scalar_ref):
+def plan_kernel(where_ref, owner_ref, cycle_ref, valid_ref, word_ref, scalar_ref):
     tm_index, tile_index = where_ref[0], where_ref[1]
-    block_count = cycle_ref.shape[1]
-    chunks = block_count // LANE
+    chunks = cycle_ref.shape[0] // LANE
     slots = owner_ref.shape[0]
-    list_rows = block_ref.shape[0]
-    owner = owner_ref[...]
+    list_rows = word_ref.shape[0]
     slot = lax.broadcasted_iota(jnp.int32, (slots, LANE), 0)
     mine = (slot % 2 == tile_index).astype(jnp.float32)
+    owner = jnp.zeros((slots, LANE), jnp.int32)
+    for s in range(slots):
+        owner = jnp.where(slot == s, owner_ref[s], owner)
 
     member, weighted = [], []
     for k in range(chunks):
         cut = slice(k * LANE, (k + 1) * LANE)
-        hit = (cycle_ref[:, cut] == owner).astype(jnp.float32)
+        hit = (cycle_ref[cut].reshape(1, LANE) == owner).astype(jnp.float32)
         member.append(hit)
-        weighted.append(hit * valid_ref[:, cut].astype(jnp.float32))
+        weighted.append(hit * valid_ref[cut].reshape(1, LANE).astype(jnp.float32))
     stacked = jnp.concatenate(member + weighted, axis=0).astype(jnp.bfloat16)
     before = lax.broadcasted_iota(jnp.int32, (LANE, 2 * LANE), 0)
     column = lax.broadcasted_iota(jnp.int32, (LANE, 2 * LANE), 1)
@@ -43,78 +45,88 @@
         low = slice(k * slots, (k + 1) * slots)
         high = slice((chunks + k) * slots, (chunks + k + 1) * slots)
         rank.append(count + sums[low, :LANE])
-        start.append(jnp.sum(member[k] * (pixels + sums[high, :LANE]), axis=0, keepdims=True))
+        start.append(pixels + sums[high, :LANE])
         count = count + sums[low, LANE:]
         pixels = pixels + sums[high, LANE:]
 
-    row = lax.broadcasted_iota(jnp.int32, (slots, slots), 0)
+    rows = (jnp.max(pixels).astype(jnp.int32) + LANE - 1) // LANE
+    rung = jnp.int32(0)
+    size = jnp.int32(LADDER[0])
+    for smaller, larger in zip(LADDER[:-1], LADDER[1:]):
+        rung = rung + (rows > smaller).astype(jnp.int32)
+        size = jnp.where(rows > smaller, larger, size)
+
+    last = slots // 2 - 1
+    order = (slot // 2) ^ tm_index ^ last
+    row = lax.broadcasted_iota(jnp.int32, (slots, slots), 0) // 2
     col = lax.broadcasted_iota(jnp.int32, (slots, slots), 1)
-    earlier = ((col < row) & (col % 2 == tile_index)).astype(jnp.float32)
+    earlier = ((col // 2) ^ tm_index ^ last) < (row ^ tm_index ^ last)
+    earlier = (earlier & (col % 2 == tile_index)).astype(jnp.float32)
     base = jnp.dot(
         earlier, count, precision=lax.Precision.HIGHEST, preferred_element_type=jnp.float32
     )
+    begin = (order * size * LANE).astype(jnp.float32)
 
     list_row = lax.broadcasted_iota(jnp.int32, (list_rows, LANE), 0)
     list_col = lax.broadcasted_iota(jnp.int32, (LANE, LANE), 0)
     lane = lax.broadcasted_iota(jnp.int32, (1, LANE), 1)
-    half_slot = (slot // 2).astype(jnp.float32)
     lists = jnp.zeros((4 * list_rows, LANE), jnp.float32)
     for k in range(chunks):
         own = member[k] * mine
         place = jnp.sum(own * (rank[k] + base), axis=0, keepdims=True).astype(jnp.int32)
-        target = jnp.sum(own * half_slot, axis=0, keepdims=True).astype(jnp.int32)
+        at = jnp.sum(own * (start[k] + begin), axis=0, keepdims=True).astype(jnp.int32)
         used = jnp.sum(own, axis=0, keepdims=True) > 0
-        begin = start[k].astype(jnp.int32)
-        block = k * LANE + lane
+        word = at * 4096 + (k * LANE + lane)
         at_row = list_row == jnp.where(used, place // LANE, -1)
         at_col = (list_col == place % LANE).astype(jnp.float32).astype(jnp.bfloat16)
-        parts = (block % 256, block // 256 + 16 * target, begin % 256, begin // 256)
         spread = jnp.concatenate(
-            [jnp.where(at_row, part.astype(jnp.float32), 0.0) for part in parts], axis=0
+            [
+                jnp.where(at_row, ((word >> (8 * part)) & 255).astype(jnp.float32), 0.0)
+                for part in range(4)
+            ],
+            axis=0,
         ).astype(jnp.bfloat16)
         lists = lists + lax.dot_general(spread, at_col, NT, preferred_element_type=jnp.float32)
     lists = lists.astype(jnp.int32)
-    block_ref[...] = lists[:list_rows] + 256 * lists[list_rows : 2 * list_rows]
-    start_ref[...] = lists[2 * list_rows : 3 * list_rows] + 256 * lists[3 * list_rows :]
-
-    most = jnp.max(pixels).astype(jnp.int32)
-    rows = (most + LANE - 1) // LANE
-    rung = jnp.int32(0)
-    for size in LADDER[:-1]:
-        rung = rung + (rows > size).astype(jnp.int32)
+    words = jnp.zeros((list_rows, LANE), jnp.int32)
+    for part in range(4):
+        words = words + (lists[part * list_rows : (part + 1) * list_rows] << (8 * part))
+    word_ref[...] = words
+
     own_slot = 2 * tm_index + tile_index
     scalar_ref[0] = rung
     scalar_ref[1] = jnp.sum(count[:, :1] * mine[:, :1]).astype(jnp.int32)
     scalar_ref[2] = jnp.sum(jnp.where(slot == own_slot, pixels, 0.0)[:, :1]).astype(jnp.int32)
     scalar_ref[3] = tile_index
-
-
-def pack_kernel(size, block_ref, start_ref, scalar_ref, near_ref, far_ref, out_ref, pool, stage):
+    scalar_ref[4] = tm_index
+
+
+def pack_kernel(word_ref, scalar_ref, near_ref, far_ref, *rest):
+    out_refs, (pool, stage) = rest[:-2], rest[-2:]
     frames, half, _ = near_ref.shape
+    stride = 2 * half + 1
     near_at = scalar_ref[3] * half
     far_at = half - near_at
-    step = 64
     for source, at in ((near_ref, near_at), (far_ref, far_at)):
         for f in range(frames):
 
             def widen(i, _, source=source, at=at, f=f):
-                begin = pl.multiple_of(i * step, step)
-                to = pl.multiple_of(f * 2 * half + at + begin, 8)
-                pool[pl.ds(to, step), :] = source[f, pl.ds(begin, step), :].astype(jnp.float32)
+                begin = pl.multiple_of(i * STEP, STEP)
+                to = f * stride + pl.multiple_of(at + begin, 8)
+                pool[pl.ds(to, STEP), :] = source[f, pl.ds(begin, STEP), :].astype(jnp.float32)
                 return 0
 
-            lax.fori_loop(0, half // step, widen, 0)
+            lax.fori_loop(0, half // STEP, widen, 0)
 
     lane = lax.broadcasted_iota(jnp.int32, (frames, LANE), 1)
 
     def place(i, carry):
         held, spill, last = carry
-        word = block_ref[i]
-        begin = start_ref[i]
+        word = word_ref[i]
         block = word & 4095
-        row = (word >> 12) * size + (begin >> 7)
-        shift = begin & (LANE - 1)
-        x = pool[pl.ds(block, frames, stride=2 * half), :]
+        row = word >> 19
+        shift = (word >> 12) & (LANE - 1)
+        x = pool[pl.ds(block, frames, stride=stride), :]
         turned = pltpu.roll(x, shift, 1)
         held = jnp.where(lane >= shift, turned, jnp.where(row == last, held, spill))
         at = pl.multiple_of(row * frames, frames)
@@ -132,26 +144,29 @@
     carry = lax.fori_loop(0, total // UNROLL, group, (zero, zero, jnp.int32(-1)))
     lax.fori_loop(total // UNROLL * UNROLL, total, place, carry)
 
-    depth = size * frames
-    for d in range(out_ref.shape[0]):
-        out_ref[d] = stage[d * depth : (d + 1) * depth, :].astype(jnp.bfloat16)
-
-
-def gram_kernel(scalar_ref, x_ref, out_ref):
-    sources = x_ref.shape[0]
+    depth = out_refs[0].shape[0]
+    for d, out_ref in enumerate(out_refs):
+        out_ref[...] = stage[d * depth : (d + 1) * depth, :].astype(jnp.bfloat16)
+
+
+def gram_kernel(scalar_ref, *refs):
+    x_refs, (out_ref, turn) = refs[:-2], refs[-2:]
+    sources = len(x_refs)
     frames = out_ref.shape[0]
     local = frames // sources
     pixels = scalar_ref[2]
+    tm_index = scalar_ref[4]
     lane = lax.broadcasted_iota(jnp.int32, (1, LANE), 1)
 
     def pair(j, carry):
         gram, total = carry
-        both = x_ref[:, pl.ds(pl.multiple_of(j * 2 * local, 2 * local), 2 * local), :]
-        both = both.astype(jnp.float32).reshape(sources, 2, local, LANE)
+        rows = pl.ds(pl.multiple_of(j * 2 * local, 2 * local), 2 * local)
+        both = [ref[rows, :].astype(jnp.float32) for ref in x_refs]
         exact, high, low = [], [], []
         for i in range(2):
             used = lane + (2 * j + i) * LANE < pixels
-            x = jnp.where(used, both[:, i].reshape(frames, LANE), 0.0)
+            x = jnp.concatenate([part[i * local : (i + 1) * local] for part in both], axis=0)
+            x = jnp.where(used, x, 0.0)
             mean = jnp.where(used, jnp.sum(x, axis=0, keepdims=True) / frames, 1.0)
             scale = 1.0 / mean
             total = total + x * scale
@@ -167,9 +182,22 @@
         gram = gram + lax.dot_general(left, right, NT, preferred_element_type=jnp.float32)
         return gram, total
 
-    start = (jnp.zeros((frames, 2 * frames), jnp.float32), jnp.zeros((frames, LANE), jnp.float32))
-    gram, total = lax.fori_loop(0, (pixels + 2 * LANE - 1) // (2 * LANE), pair, start)
-    gram = gram[:, :frames] + gram[:, frames:]
+    def two_pairs(j, carry):
+        return pair(2 * j + 1, pair(2 * j, carry))
+
+    def in_order(value):
+        for j in range(sources):
+            at = pl.multiple_of((tm_index ^ (sources - 1 - j)) * local, local)
+            turn[pl.ds(at, local), :] = value[j * local : (j + 1) * local]
+        return turn[...]
+
+    carry = (jnp.zeros((frames, 2 * frames), jnp.float32), jnp.zeros((frames, LANE), jnp.float32))
+    pairs = (pixels + 2 * LANE - 1) // (2 * LANE)
+    carry = lax.fori_loop(0, pairs // 2, two_pairs, carry)
+    gram, total = lax.fori_loop(pairs // 2 * 2, pairs, pair, carry)
+    gram = in_order(gram[:, :frames] + gram[:, frames:])
+    gram = in_order(gram.T)
+    total = in_order(total)
     first = jnp.sum(total, axis=1, keepdims=True)
     second = jnp.sum(total.T, axis=0, keepdims=True)
     out_ref[...] = pixels.astype(jnp.float32) * gram / (first * second)
@@ -178,62 +206,63 @@
 def on_device_routed(frames, block_cycle, block_valid, cycle_owner):
     tm_count = lax.axis_size("tm")
     local_frames, half, _ = frames.shape
-    block_count = block_cycle.shape[0]
-    slots = cycle_owner.shape[0]
-    list_rows = -(-block_count // (8 * LANE)) * 8
+    list_rows = -(-block_cycle.shape[0] // (8 * LANE)) * 8
     vmem = pl.BlockSpec(memory_space=pltpu.VMEM)
     smem = pl.BlockSpec(memory_space=pltpu.SMEM)
     params = pltpu.CompilerParams(vmem_limit_bytes=VMEM_LIMIT)
 
     far = lax.ppermute(frames, "tile", [(0, 1), (1, 0)])
     where = jnp.stack([lax.axis_index("tm"), lax.axis_index("tile")]).astype(jnp.int32)
-    block_list, start_list, scalars = pl.pallas_call(
+    words, scalars = pl.pallas_call(
         plan_kernel,
         out_shape=(
             jax.ShapeDtypeStruct((list_rows, LANE), jnp.int32),
-            jax.ShapeDtypeStruct((list_rows, LANE), jnp.int32),
-            jax.ShapeDtypeStruct((4,), jnp.int32),
+            jax.ShapeDtypeStruct((5,), jnp.int32),
         ),
-        in_specs=[smem, vmem, vmem, vmem],
-        out_specs=(vmem, vmem, smem),
+        in_specs=[smem, smem, vmem, vmem],
+        out_specs=(vmem, smem),
         compiler_params=params,
         name="plan",
-    )(where, block_cycle[None, :], block_valid[None, :], cycle_owner[:, None])
-    block_list = block_list.reshape(-1)
-    start_list = start_list.reshape(-1)
+    )(where, cycle_owner, block_cycle, block_valid)
+    words = words.reshape(-1)
 
     def branch(size):
-        def run(block_list, start_list, scalars, near, far):
+        depth = size * local_frames
+
+        def run(words, scalars, near, far):
             send = pl.pallas_call(
-                functools.partial(pack_kernel, size),
-                out_shape=jax.ShapeDtypeStruct(
-                    (tm_count, size * local_frames, LANE), jnp.bfloat16
-                ),
-                in_specs=[smem, smem, smem, vmem, vmem],
-                out_specs=vmem,
+                pack_kernel,
+                out_shape=(jax.ShapeDtypeStruct((depth, LANE), jnp.bfloat16),) * tm_count,
+                in_specs=[smem, smem, vmem, vmem],
+                out_specs=(vmem,) * tm_count,
                 scratch_shapes=[
-                    pltpu.VMEM((local_frames * 2 * half, LANE), jnp.float32),
-                    pltpu.VMEM(((tm_count * size + 1) * local_frames, LANE), jnp.float32),
+                    pltpu.VMEM((local_frames * (2 * half + 1) + 8, LANE), jnp.float32),
+                    pltpu.VMEM((tm_count * depth + local_frames, LANE), jnp.float32),
                 ],
                 compiler_params=params,
                 name="pack",
-            )(block_list, start_list, scalars, near, far)
-            got = lax.all_to_all(send, "tm", split_axis=0, concat_axis=0, tiled=True)
+            )(words, scalars, near, far)
+            got = []
+            for j in range(tm_count):
+                apart = tm_count - 1 - j
+                pairs = [(i, i ^ apart) for i in range(tm_count)]
+                got.append(lax.ppermute(send[j], "tm", pairs) if apart else send[j])
             return pl.pallas_call(
                 gram_kernel,
                 out_shape=jax.ShapeDtypeStruct(
                     (tm_count * local_frames, tm_count * local_frames), jnp.float32
                 ),
-                in_specs=[smem, vmem],
+                in_specs=[smem] + [vmem] * tm_count,
                 out_specs=vmem,
+                scratch_shapes=[pltpu.VMEM((tm_count * local_frames, LANE), jnp.float32)],
                 compiler_params=params,
                 name="gram",
-            )(scalars, got)
+            )(scalars, *got)
 
         return run
 
     return lax.switch(
-        scalars[0], [branch(size) for size in LADDER], block_list, start_list, scalars, frames, far
+        scalars[0], [branch(size) for size in LADDER], words, scalars, frames, far
     )
 
 

time: 72.2 us -> 68.1 us (0.943); the launches traced: 71.9 us -> 67 us
  blocking collectives: 42.1 us -> 0 us
  starting transfers between devices: 0.45 us -> 35.4 us
  waiting for transfers between devices: 0.26 us -> 8.76 us
  Pallas kernels: 26.1 us -> 19.5 us
    all_to_all x1 -> x0, blocking collectives: 42.1 us -> none  [run(): got = lax.all_to_all(send, 'tm', split_axis=0, concat_axis=0, tiled=True)]
    ppermute x0 -> x15, starting transfers between devices: none -> 35 us  [run(): got.append(lax.ppermute(send[j], 'tm', pairs) if apart else send[j])]
    ppermute x0 -> x15, waiting for transfers between devices: none -> 8.36 us  [run(): got.append(lax.ppermute(send[j], 'tm', pairs) if apart else send[j])]
    pallas_call x1, Pallas kernels: 18.9 us -> 14.1 us  [run(): pl.pallas_call(pack_kernel, out_shape=(jax.ShapeDtypeStruct((depth, LANE)...]
    broadcast_in_dim x3 -> x0, local copies, waits for them, and re-layouts: 2.16 us -> none  [the longest x1 0.74 us: on_device_routed(): cycle_owner[:, None]]
    unnamed x2 -> x8, local copies, waits for them, and re-layouts: 0.62 us -> 2.69 us
    pallas_call x1, Pallas kernels: 5.3 us -> 3.58 us  [run(): pl.pallas_call(gram_kernel, out_shape=jax.ShapeDtypeStruct((tm_count * lo...]
  transfers between devices with their start and end apart: 1 -> 16, of which waited for: 1 -> 9; matrix products, arithmetic and copies ran while one was open for 3% -> 0% of each run, Pallas kernels for 3% -> 3%
where the time goes in v2:
time: 68.1 us; the launch traced here: 67 us
  starting transfers between devices  35.4 us (52%)
  Pallas kernels  19.5 us (29%)
  waiting for transfers between devices  8.76 us (13%)
  local copies, waits for them, and re-layouts  2.69 us (4%)
    ppermute x15, starting transfers between devices, run(): got.append(lax.ppermute(send[j], 'tm', pairs) if apart else send[j])  35 us
    pallas_call x1, Pallas kernels, run(): pl.pallas_call(pack_kernel, out_shape=(jax.ShapeDtypeStruct((depth, LANE)...  14.1 us
    ppermute x15, waiting for transfers between devices, run(): got.append(lax.ppermute(send[j], 'tm', pairs) if apart else send[j])  8.36 us
    pallas_call x1, Pallas kernels, run(): pl.pallas_call(gram_kernel, out_shape=jax.ShapeDtypeStruct((tm_count * lo...  3.58 us
    unnamed x8, local copies, waits for them, and re-layouts  2.69 us
    pallas_call x1, Pallas kernels, on_device_routed(): pl.pallas_call(plan_kernel, out_shape=(jax.ShapeDtypeStruct((list_rows, L...  1.78 us
  transfers between devices with their start and end apart: 16, of which 9 were waited for; matrix products, arithmetic and copies ran while one was open for 0% of the time, Pallas kernels for 3%

profile of v2, /device:TPU:0, one launch (start us, length us, event | category | flops | bytes accessed | tf_op | source)
XLA Modules:
  0.0 67.0 jit_solution(10972244494040191329)
XLA Ops:
  0.0 0.5 collective-permute-start.225
  0.5 0.7 %copy-done = s32[2304]{0:T(1024)S(1)} copy-done((s32[2304]{0:T(1024)S(1)}, s32[2304]{0:T(1024)}, u32[]{:S(2)}) %copy-start) | copy-done | bytes 9240
  1.2 0.7 %copy-done.1 = s32[2304]{0:T(1024)S(1)} copy-done((s32[2304]{0:T(1024)S(1)}, s32[2304]{0:T(1024)}, u32[]{:S(2)}) %copy-start.1) | copy-done | bytes 9240
  1.9 0.7 copy-done.2
  2.6 1.8 %plan.1 = (s32[24,128]{1,0:T(8,128)S(1)}, s32[5]{0:T(128)S(1)}) custom-call(s32[2]{0:T(128)S(1)} %pad_add_fusion.where_ref, s32[32]{0:T(128)S(1)} %copy-done.2, s32[2304]{0:T(1024)S(1)} %copy-done, s32[2304]{0:T(1024)S(1)} %copy-done.1), custom_call_target="tpu_custom_call" | custom-call | tf_op jit(solution)/shard_map/plan/pallas_call | solution.py:216
  4.4 0.4 collective-permute-done.225
  4.8 61.5 %conditional.1 = (f32[128,128]{1,0:T(8,128)S(1)}) conditional(s32[]{:T(128)} %bitcast.17, (s32[24,128]{1,0:T(8,128)S(1)}, s32[5]{0:T(128)S(1)}, bf16[8,1152,128]{2,1,0:T(8,128)(2,1)}, bf16[8,1152,128]{2,1,0:T(8,128)(2,1)S(1)}) %tuple.50, (s32[24,128]{1,0:T(8,128)S(1)}, s32[5]{0:T(128)S(1)}, ...), branch_computations={%region_0.0_spmd, %region_1.0_spmd, %region_2.0_spmd, %region_3.0_... | conditional | bytes 17695328 | solution.py:264
  4.8 14.1 %pack.19 = (bf16[320,128]{1,0:T(8,128)(2,1)S(1)}, bf16[320,128]{1,0:T(8,128)(2,1)S(1)}, bf16[320,128]{1,0:T(8,128)(2,1)S(1)}, bf16[320,128]{1,0:T(8,128)(2,1)S(1...) custom-call(s32[3072]{0:T(1024)S(1)} %bitcast.23, ...), custom_call_target="tpu_custom_call" | custom-call | tf_op jit(solution)/shard_map/cond/branch_4_fun/pack/pallas_call | solution.py:233
  19.0 6.9 %collective-permute-start.60 = (bf16[320,128]{1,0:T(8,128)(2,1)S(1)}, bf16[320,128]{1,0:T(8,128)(2,1)S(1)}, u32[]{:S(2)}, u32[]{:S(2)}) collective-permute-start(bf16[320,128]{1,0:T(8,128)(2,1)S(1)} %get-tuple-element.225), channel_id=1, source_target_pairs={{0,30},{2,28},{4,26},{6,24},{8,22},{10,20},{12,18},{14,16},{16,14}... | collective-permute-start | bytes 245768 | tf_op jit(solution)/shard_map/cond/branch_4_fun/ppermute | solution.py:249
  25.9 0.2 collective-permute-start.61
  26.0 3.6 %collective-permute-start.62 = (bf16[320,128]{1,0:T(8,128)(2,1)S(1)}, bf16[320,128]{1,0:T(8,128)(2,1)S(1)}, u32[]{:S(2)}, u32[]{:S(2)}) collective-permute-start(bf16[320,128]{1,0:T(8,128)(2,1)S(1)} %get-tuple-element.227), channel_id=1, source_target_pairs={{0,26},{2,24},{4,30},{6,28},{8,18},{10,16},{12,22},{14,20},{16,10}... | collective-permute-start | bytes 245768 | tf_op jit(solution)/shard_map/cond/branch_4_fun/ppermute | solution.py:249
  29.6 0.2 collective-permute-start.63
  29.8 0.9 %collective-permute-start.64 = (bf16[320,128]{1,0:T(8,128)(2,1)S(1)}, bf16[320,128]{1,0:T(8,128)(2,1)S(1)}, u32[]{:S(2)}, u32[]{:S(2)}) collective-permute-start(bf16[320,128]{1,0:T(8,128)(2,1)S(1)} %get-tuple-element.229), channel_id=1, source_target_pairs={{0,22},{2,20},{4,18},{6,16},{8,30},{10,28},{12,26},{14,24},{16,6},... | collective-permute-start | bytes 245768 | tf_op jit(solution)/shard_map/cond/branch_4_fun/ppermute | solution.py:249
  30.7 3.9 %collective-permute-start.65 = (bf16[320,128]{1,0:T(8,128)(2,1)S(1)}, bf16[320,128]{1,0:T(8,128)(2,1)S(1)}, u32[]{:S(2)}, u32[]{:S(2)}) collective-permute-start(bf16[320,128]{1,0:T(8,128)(2,1)S(1)} %get-tuple-element.230), channel_id=1, source_target_pairs={{0,20},{2,22},{4,16},{6,18},{8,28},{10,30},{12,24},{14,26},{16,4},... | collective-permute-start | bytes 245768 | tf_op jit(solution)/shard_map/cond/branch_4_fun/ppermute | solution.py:249
  34.6 7.6 %collective-permute-start.66 = (bf16[320,128]{1,0:T(8,128)(2,1)S(1)}, bf16[320,128]{1,0:T(8,128)(2,1)S(1)}, u32[]{:S(2)}, u32[]{:S(2)}) collective-permute-start(bf16[320,128]{1,0:T(8,128)(2,1)S(1)} %get-tuple-element.231), channel_id=1, source_target_pairs={{0,18},{2,16},{4,22},{6,20},{8,26},{10,24},{12,30},{14,28},{16,2},... | collective-permute-start | bytes 245768 | tf_op jit(solution)/shard_map/cond/branch_4_fun/ppermute | solution.py:249
  42.2 4.1 %collective-permute-start.67 = (bf16[320,128]{1,0:T(8,128)(2,1)S(1)}, bf16[320,128]{1,0:T(8,128)(2,1)S(1)}, u32[]{:S(2)}, u32[]{:S(2)}) collective-permute-start(bf16[320,128]{1,0:T(8,128)(2,1)S(1)} %get-tuple-element.232), channel_id=1, source_target_pairs={{0,16},{2,18},{4,20},{6,22},{8,24},{10,26},{12,28},{14,30},{16,0},... | collective-permute-start | bytes 245768 | tf_op jit(solution)/shard_map/cond/branch_4_fun/ppermute | solution.py:249
  46.3 0.9 %collective-permute-start.68 = (bf16[320,128]{1,0:T(8,128)(2,1)S(1)}, bf16[320,128]{1,0:T(8,128)(2,1)S(1)}, u32[]{:S(2)}, u32[]{:S(2)}) collective-permute-start(bf16[320,128]{1,0:T(8,128)(2,1)S(1)} %get-tuple-element.233), channel_id=1, source_target_pairs={{0,14},{2,12},{4,10},{6,8},{8,6},{10,4},{12,2},{14,0},{16,30},{18,... | collective-permute-start | bytes 245768 | tf_op jit(solution)/shard_map/cond/branch_4_fun/ppermute | solution.py:249
  47.1 0.7 collective-permute-done.64.refs_4_
  47.8 1.1 %collective-permute-start.69 = (bf16[320,128]{1,0:T(8,128)(2,1)S(1)}, bf16[320,128]{1,0:T(8,128)(2,1)S(1)}, u32[]{:S(2)}, u32[]{:S(2)}) collective-permute-start(bf16[320,128]{1,0:T(8,128)(2,1)S(1)} %get-tuple-element.234), channel_id=1, source_target_pairs={{0,12},{2,14},{4,8},{6,10},{8,4},{10,6},{12,0},{14,2},{16,28},{18,... | collective-permute-start | bytes 245768 | tf_op jit(solution)/shard_map/cond/branch_4_fun/ppermute | solution.py:249
  48.9 2.5 %collective-permute-done.65.refs_5_ = bf16[320,128]{1,0:T(8,128)(2,1)S(1)} collective-permute-done((bf16[320,128]{1,0:T(8,128)(2,1)S(1)}, bf16[320,128]{1,0:T(8,128)(2,1)S(1)}, u32[]{:S(2)}, u32[]{:S(2)}) %collective-permute-start.65) | collective-permute-done | bytes 81952 | tf_op jit(solution)/shard_map/cond/branch_4_fun/ppermute | solution.py:249
  51.4 2.3 %collective-permute-start.70 = (bf16[320,128]{1,0:T(8,128)(2,1)S(1)}, bf16[320,128]{1,0:T(8,128)(2,1)S(1)}, u32[]{:S(2)}, u32[]{:S(2)}) collective-permute-start(bf16[320,128]{1,0:T(8,128)(2,1)S(1)} %get-tuple-element.235), channel_id=1, source_target_pairs={{0,10},{2,8},{4,14},{6,12},{8,2},{10,0},{12,6},{14,4},{16,26},{18,... | collective-permute-start | bytes 245768 | tf_op jit(solution)/shard_map/cond/branch_4_fun/ppermute | solution.py:249
  53.7 0.6 collective-permute-done.67.refs_7_
  54.3 1.7 %collective-permute-start.72 = (bf16[320,128]{1,0:T(8,128)(2,1)S(1)}, bf16[320,128]{1,0:T(8,128)(2,1)S(1)}, u32[]{:S(2)}, u32[]{:S(2)}) collective-permute-start(bf16[320,128]{1,0:T(8,128)(2,1)S(1)} %get-tuple-element.237), channel_id=1, source_target_pairs={{0,6},{2,4},{4,2},{6,0},{8,14},{10,12},{12,10},{14,8},{16,22},{18,... | collective-permute-start | bytes 245768 | tf_op jit(solution)/shard_map/cond/branch_4_fun/ppermute | solution.py:249
  56.0 0.4 collective-permute-start.73
  56.4 1.5 %collective-permute-done.69.refs_9_ = bf16[320,128]{1,0:T(8,128)(2,1)S(1)} collective-permute-done((bf16[320,128]{1,0:T(8,128)(2,1)S(1)}, bf16[320,128]{1,0:T(8,128)(2,1)S(1)}, u32[]{:S(2)}, u32[]{:S(2)}) %collective-permute-start.69) | collective-permute-done | bytes 81952 | tf_op jit(solution)/shard_map/cond/branch_4_fun/ppermute | solution.py:249
  57.8 1.3 %collective-permute-start.74 = (bf16[320,128]{1,0:T(8,128)(2,1)S(1)}, bf16[320,128]{1,0:T(8,128)(2,1)S(1)}, u32[]{:S(2)}, u32[]{:S(2)}) collective-permute-start(bf16[320,128]{1,0:T(8,128)(2,1)S(1)} %get-tuple-element.239), channel_id=1, source_target_pairs={{0,2},{2,0},{4,6},{6,4},{8,10},{10,8},{12,14},{14,12},{16,18},{18,... | collective-permute-start | bytes 245768 | tf_op jit(solution)/shard_map/cond/branch_4_fun/ppermute | solution.py:249
  59.2 0.9 %collective-permute-done.71.refs_11_ = bf16[320,128]{1,0:T(8,128)(2,1)S(1)} collective-permute-done((bf16[320,128]{1,0:T(8,128)(2,1)S(1)}, bf16[320,128]{1,0:T(8,128)(2,1)S(1)}, u32[]{:S(2)}, u32[]{:S(2)}) %collective-permute-start.71) | collective-permute-done | bytes 81952 | tf_op jit(solution)/shard_map/cond/branch_4_fun/ppermute | solution.py:249
  60.1 0.7 %collective-permute-done.72.refs_12_ = bf16[320,128]{1,0:T(8,128)(2,1)S(1)} collective-permute-done((bf16[320,128]{1,0:T(8,128)(2,1)S(1)}, bf16[320,128]{1,0:T(8,128)(2,1)S(1)}, u32[]{:S(2)}, u32[]{:S(2)}) %collective-permute-start.72) | collective-permute-done | bytes 81952 | tf_op jit(solution)/shard_map/cond/branch_4_fun/ppermute | solution.py:249
  60.8 0.3 collective-permute-done.73.refs_13_
  61.1 1.2 %collective-permute-done.74.refs_14_ = bf16[320,128]{1,0:T(8,128)(2,1)S(1)} collective-permute-done((bf16[320,128]{1,0:T(8,128)(2,1)S(1)}, bf16[320,128]{1,0:T(8,128)(2,1)S(1)}, u32[]{:S(2)}, u32[]{:S(2)}) %collective-permute-start.74) | collective-permute-done | bytes 81952 | tf_op jit(solution)/shard_map/cond/branch_4_fun/ppermute | solution.py:249
  62.3 3.6 %gram.19 = f32[128,128]{1,0:T(8,128)S(1)} custom-call(s32[5]{0:T(128)S(1)} %get-tuple-element.221.scalar_ref, bf16[320,128]{1,0:T(8,128)(2,1)S(1)} %collective-permute-done.60.refs_0_, bf16[320,128]{1,0:T(8,128)(2,1)S(1)} %collective-permute-done.61.refs_1_, bf16[320,128]{1,0:T(8,128)(2,1)S(1)} %collective-permute-done.62.refs_2_, ...), custom_call_target="tpu_custom_call" | custom-call | tf_op jit(solution)/shard_map/cond/branch_4_fun/gram/pallas_call | solution.py:250
  66.3 0.6 copy-done.3
  (13 shorter events, 0.1 us)
Async XLA Ops:
  0.0 4.8 %collective-permute-start.225 = (bf16[8,1152,128]{2,1,0:T(8,128)(2,1)}, bf16[8,1152,128]{2,1,0:T(8,128)(2,1)S(1)}, u32[]{:S(2)}, u32[]{:S(2)}) collective-permute-start(bf16[8,1152,128]{2,1,0:T(8,128)(2,1)} %param.19), channel_id=1, source_target_pairs={{0,1},{1,0},{2,3},{3,2},{4,5},{5,4},{6,7},{7,6},{8,9},{9,8},{10,11... | collective-permute-start | bytes 7077896 | tf_op jit(solution)/shard_map/ppermute | solution.py:214
  0.5 0.7 %copy-start = (s32[2304]{0:T(1024)S(1)}, s32[2304]{0:T(1024)}, u32[]{:S(2)}) copy-start(s32[2304]{0:T(1024)} %cycle_ref.1) | copy-start | bytes 27652
  1.2 0.7 %copy-start.1 = (s32[2304]{0:T(1024)S(1)}, s32[2304]{0:T(1024)}, u32[]{:S(2)}) copy-start(s32[2304]{0:T(1024)} %valid_ref.1) | copy-start | bytes 27652
  1.9 0.7 copy-start.2
  19.0 11.8 %collective-permute-start.60 = (bf16[320,128]{1,0:T(8,128)(2,1)S(1)}, bf16[320,128]{1,0:T(8,128)(2,1)S(1)}, u32[]{:S(2)}, u32[]{:S(2)}) collective-permute-start(bf16[320,128]{1,0:T(8,128)(2,1)S(1)} %get-tuple-element.225), channel_id=1, source_target_pairs={{0,30},{2,28},{4,26},{6,24},{8,22},{10,20},{12,18},{14,16},{16,14}... | collective-permute-start | bytes 245768 | tf_op jit(solution)/shard_map/cond/branch_4_fun/ppermute | solution.py:249
  25.9 8.7 %collective-permute-start.61 = (bf16[320,128]{1,0:T(8,128)(2,1)S(1)}, bf16[320,128]{1,0:T(8,128)(2,1)S(1)}, u32[]{:S(2)}, u32[]{:S(2)}) collective-permute-start(bf16[320,128]{1,0:T(8,128)(2,1)S(1)} %get-tuple-element.226), channel_id=1, source_target_pairs={{0,28},{2,30},{4,24},{6,26},{8,20},{10,22},{12,16},{14,18},{16,12}... | collective-permute-start | bytes 245768 | tf_op jit(solution)/shard_map/cond/branch_4_fun/ppermute | solution.py:249
  26.0 16.1 %collective-permute-start.62 = (bf16[320,128]{1,0:T(8,128)(2,1)S(1)}, bf16[320,128]{1,0:T(8,128)(2,1)S(1)}, u32[]{:S(2)}, u32[]{:S(2)}) collective-permute-start(bf16[320,128]{1,0:T(8,128)(2,1)S(1)} %get-tuple-element.227), channel_id=1, source_target_pairs={{0,26},{2,24},{4,30},{6,28},{8,18},{10,16},{12,22},{14,20},{16,10}... | collective-permute-start | bytes 245768 | tf_op jit(solution)/shard_map/cond/branch_4_fun/ppermute | solution.py:249
  29.6 16.7 %collective-permute-start.63 = (bf16[320,128]{1,0:T(8,128)(2,1)S(1)}, bf16[320,128]{1,0:T(8,128)(2,1)S(1)}, u32[]{:S(2)}, u32[]{:S(2)}) collective-permute-start(bf16[320,128]{1,0:T(8,128)(2,1)S(1)} %get-tuple-element.228), channel_id=1, source_target_pairs={{0,24},{2,26},{4,28},{6,30},{8,16},{10,18},{12,20},{14,22},{16,8},... | collective-permute-start | bytes 245768 | tf_op jit(solution)/shard_map/cond/branch_4_fun/ppermute | solution.py:249
  29.8 18.0 %collective-permute-start.64 = (bf16[320,128]{1,0:T(8,128)(2,1)S(1)}, bf16[320,128]{1,0:T(8,128)(2,1)S(1)}, u32[]{:S(2)}, u32[]{:S(2)}) collective-permute-start(bf16[320,128]{1,0:T(8,128)(2,1)S(1)} %get-tuple-element.229), channel_id=1, source_target_pairs={{0,22},{2,20},{4,18},{6,16},{8,30},{10,28},{12,26},{14,24},{16,6},... | collective-permute-start | bytes 245768 | tf_op jit(solution)/shard_map/cond/branch_4_fun/ppermute | solution.py:249
  30.7 20.7 %collective-permute-start.65 = (bf16[320,128]{1,0:T(8,128)(2,1)S(1)}, bf16[320,128]{1,0:T(8,128)(2,1)S(1)}, u32[]{:S(2)}, u32[]{:S(2)}) collective-permute-start(bf16[320,128]{1,0:T(8,128)(2,1)S(1)} %get-tuple-element.230), channel_id=1, source_target_pairs={{0,20},{2,22},{4,16},{6,18},{8,28},{10,30},{12,24},{14,26},{16,4},... | collective-permute-start | bytes 245768 | tf_op jit(solution)/shard_map/cond/branch_4_fun/ppermute | solution.py:249
  34.6 19.1 %collective-permute-start.66 = (bf16[320,128]{1,0:T(8,128)(2,1)S(1)}, bf16[320,128]{1,0:T(8,128)(2,1)S(1)}, u32[]{:S(2)}, u32[]{:S(2)}) collective-permute-start(bf16[320,128]{1,0:T(8,128)(2,1)S(1)} %get-tuple-element.231), channel_id=1, source_target_pairs={{0,18},{2,16},{4,22},{6,20},{8,26},{10,24},{12,30},{14,28},{16,2},... | collective-permute-start | bytes 245768 | tf_op jit(solution)/shard_map/cond/branch_4_fun/ppermute | solution.py:249
  42.2 12.2 %collective-permute-start.67 = (bf16[320,128]{1,0:T(8,128)(2,1)S(1)}, bf16[320,128]{1,0:T(8,128)(2,1)S(1)}, u32[]{:S(2)}, u32[]{:S(2)}) collective-permute-start(bf16[320,128]{1,0:T(8,128)(2,1)S(1)} %get-tuple-element.232), channel_id=1, source_target_pairs={{0,16},{2,18},{4,20},{6,22},{8,24},{10,26},{12,28},{14,30},{16,0},... | collective-permute-start | bytes 245768 | tf_op jit(solution)/shard_map/cond/branch_4_fun/ppermute | solution.py:249
  46.3 9.7 %collective-permute-start.68 = (bf16[320,128]{1,0:T(8,128)(2,1)S(1)}, bf16[320,128]{1,0:T(8,128)(2,1)S(1)}, u32[]{:S(2)}, u32[]{:S(2)}) collective-permute-start(bf16[320,128]{1,0:T(8,128)(2,1)S(1)} %get-tuple-element.233), channel_id=1, source_target_pairs={{0,14},{2,12},{4,10},{6,8},{8,6},{10,4},{12,2},{14,0},{16,30},{18,... | collective-permute-start | bytes 245768 | tf_op jit(solution)/shard_map/cond/branch_4_fun/ppermute | solution.py:249
  47.8 10.0 %collective-permute-start.69 = (bf16[320,128]{1,0:T(8,128)(2,1)S(1)}, bf16[320,128]{1,0:T(8,128)(2,1)S(1)}, u32[]{:S(2)}, u32[]{:S(2)}) collective-permute-start(bf16[320,128]{1,0:T(8,128)(2,1)S(1)} %get-tuple-element.234), channel_id=1, source_target_pairs={{0,12},{2,14},{4,8},{6,10},{8,4},{10,6},{12,0},{14,2},{16,28},{18,... | collective-permute-start | bytes 245768 | tf_op jit(solution)/shard_map/cond/branch_4_fun/ppermute | solution.py:249
  51.4 7.8 %collective-permute-start.70 = (bf16[320,128]{1,0:T(8,128)(2,1)S(1)}, bf16[320,128]{1,0:T(8,128)(2,1)S(1)}, u32[]{:S(2)}, u32[]{:S(2)}) collective-permute-start(bf16[320,128]{1,0:T(8,128)(2,1)S(1)} %get-tuple-element.235), channel_id=1, source_target_pairs={{0,10},{2,8},{4,14},{6,12},{8,2},{10,0},{12,6},{14,4},{16,26},{18,... | collective-permute-start | bytes 245768 | tf_op jit(solution)/shard_map/cond/branch_4_fun/ppermute | solution.py:249
  53.7 6.4 %collective-permute-start.71 = (bf16[320,128]{1,0:T(8,128)(2,1)S(1)}, bf16[320,128]{1,0:T(8,128)(2,1)S(1)}, u32[]{:S(2)}, u32[]{:S(2)}) collective-permute-start(bf16[320,128]{1,0:T(8,128)(2,1)S(1)} %get-tuple-element.236), channel_id=1, source_target_pairs={{0,8},{2,10},{4,12},{6,14},{8,0},{10,2},{12,4},{14,6},{16,24},{18,... | collective-permute-start | bytes 245768 | tf_op jit(solution)/shard_map/cond/branch_4_fun/ppermute | solution.py:249
  54.3 6.5 %collective-permute-start.72 = (bf16[320,128]{1,0:T(8,128)(2,1)S(1)}, bf16[320,128]{1,0:T(8,128)(2,1)S(1)}, u32[]{:S(2)}, u32[]{:S(2)}) collective-permute-start(bf16[320,128]{1,0:T(8,128)(2,1)S(1)} %get-tuple-element.237), channel_id=1, source_target_pairs={{0,6},{2,4},{4,2},{6,0},{8,14},{10,12},{12,10},{14,8},{16,22},{18,... | collective-permute-start | bytes 245768 | tf_op jit(solution)/shard_map/cond/branch_4_fun/ppermute | solution.py:249
  56.0 5.1 %collective-permute-start.73 = (bf16[320,128]{1,0:T(8,128)(2,1)S(1)}, bf16[320,128]{1,0:T(8,128)(2,1)S(1)}, u32[]{:S(2)}, u32[]{:S(2)}) collective-permute-start(bf16[320,128]{1,0:T(8,128)(2,1)S(1)} %get-tuple-element.238), channel_id=1, source_target_pairs={{0,4},{2,6},{4,0},{6,2},{8,12},{10,14},{12,8},{14,10},{16,20},{18,... | collective-permute-start | bytes 245768 | tf_op jit(solution)/shard_map/cond/branch_4_fun/ppermute | solution.py:249
  57.8 4.4 %collective-permute-start.74 = (bf16[320,128]{1,0:T(8,128)(2,1)S(1)}, bf16[320,128]{1,0:T(8,128)(2,1)S(1)}, u32[]{:S(2)}, u32[]{:S(2)}) collective-permute-start(bf16[320,128]{1,0:T(8,128)(2,1)S(1)} %get-tuple-element.239), channel_id=1, source_target_pairs={{0,2},{2,0},{4,6},{6,4},{8,10},{10,8},{12,14},{14,12},{16,18},{18,... | collective-permute-start | bytes 245768 | tf_op jit(solution)/shard_map/cond/branch_4_fun/ppermute | solution.py:249
  66.3 0.6 copy-start.3

commit v3 on v2

--- a/solution.py
+++ b/solution.py
@@ -8,15 +8,27 @@
 from jax.sharding import PartitionSpec as P
 
 LANE = 128
-UNROLL = 8
-STEP = 192
+UNROLL = 16
+STEP = 384
 VMEM_LIMIT = 48 * 1024 * 1024
 LADDER = (16, 24, 32, 36, 40, 42, 44, 46, 48, 52, 56, 64, 80, 104, 144)
 NT = (((1,), (1,)), ((), ()))
 
 
-def plan_kernel(where_ref, owner_ref, cycle_ref, valid_ref, word_ref, scalar_ref):
-    tm_index, tile_index = where_ref[0], where_ref[1]
+def plan_kernel(
+    owner_in, cycle_in, valid_in, word_ref, scalar_ref, owner_ref, cycle_ref, valid_ref, arrived
+):
+    tm_index, tile_index = lax.axis_index("tm"), lax.axis_index("tile")
+    fetches = [
+        pltpu.make_async_copy(source, target, arrived.at[i])
+        for i, (source, target) in enumerate(
+            ((owner_in, owner_ref), (cycle_in, cycle_ref), (valid_in, valid_ref))
+        )
+    ]
+    for fetch in fetches:
+        fetch.start()
+    for fetch in fetches:
+        fetch.wait()
     chunks = cycle_ref.shape[0] // LANE
     slots = owner_ref.shape[0]
     list_rows = word_ref.shape[0]
@@ -56,16 +68,13 @@
         rung = rung + (rows > smaller).astype(jnp.int32)
         size = jnp.where(rows > smaller, larger, size)
 
-    last = slots // 2 - 1
-    order = (slot // 2) ^ tm_index ^ last
-    row = lax.broadcasted_iota(jnp.int32, (slots, slots), 0) // 2
+    row = lax.broadcasted_iota(jnp.int32, (slots, slots), 0)
     col = lax.broadcasted_iota(jnp.int32, (slots, slots), 1)
-    earlier = ((col // 2) ^ tm_index ^ last) < (row ^ tm_index ^ last)
-    earlier = (earlier & (col % 2 == tile_index)).astype(jnp.float32)
+    earlier = ((col < row) & (col % 2 == tile_index)).astype(jnp.float32)
     base = jnp.dot(
         earlier, count, precision=lax.Precision.HIGHEST, preferred_element_type=jnp.float32
     )
-    begin = (order * size * LANE).astype(jnp.float32)
+    begin = (slot // 2 * size * LANE).astype(jnp.float32)
 
     list_row = lax.broadcasted_iota(jnp.int32, (list_rows, LANE), 0)
     list_col = lax.broadcasted_iota(jnp.int32, (LANE, LANE), 0)
@@ -98,11 +107,9 @@
     scalar_ref[1] = jnp.sum(count[:, :1] * mine[:, :1]).astype(jnp.int32)
     scalar_ref[2] = jnp.sum(jnp.where(slot == own_slot, pixels, 0.0)[:, :1]).astype(jnp.int32)
     scalar_ref[3] = tile_index
-    scalar_ref[4] = tm_index
-
-
-def pack_kernel(word_ref, scalar_ref, near_ref, far_ref, *rest):
-    out_refs, (pool, stage) = rest[:-2], rest[-2:]
+
+
+def pack_kernel(word_ref, scalar_ref, near_ref, far_ref, out_ref, pool, stage):
     frames, half, _ = near_ref.shape
     stride = 2 * half + 1
     near_at = scalar_ref[3] * half
@@ -120,48 +127,48 @@
 
     lane = lax.broadcasted_iota(jnp.int32, (frames, LANE), 1)
 
-    def place(i, carry):
+    def place(i, count, carry):
         held, spill, last = carry
-        word = word_ref[i]
-        block = word & 4095
-        row = word >> 19
-        shift = (word >> 12) & (LANE - 1)
-        x = pool[pl.ds(block, frames, stride=stride), :]
-        turned = pltpu.roll(x, shift, 1)
-        held = jnp.where(lane >= shift, turned, jnp.where(row == last, held, spill))
-        at = pl.multiple_of(row * frames, frames)
-        stage[pl.ds(at, frames), :] = held
-        stage[pl.ds(at + frames, frames), :] = turned
-        return held, turned, row
-
-    def group(j, carry):
-        for i in range(UNROLL):
-            carry = place(j * UNROLL + i, carry)
-        return carry
+        turned, row, shift = [], [], []
+        for j in range(count):
+            word = word_ref[i + j]
+            x = pool[pl.ds(word & 4095, frames, stride=stride), :]
+            row.append(word >> 19)
+            shift.append((word >> 12) & (LANE - 1))
+            turned.append(pltpu.roll(x, shift[j], 1))
+        for j in range(count):
+            held = jnp.where(
+                lane >= shift[j], turned[j], jnp.where(row[j] == last, held, spill)
+            )
+            spill, last = turned[j], row[j]
+            at = pl.multiple_of(last * frames, frames)
+            stage[pl.ds(at, frames), :] = held
+            stage[pl.ds(at + frames, frames), :] = spill
+        return held, spill, last
 
     total = scalar_ref[1]
     zero = jnp.zeros((frames, LANE), jnp.float32)
-    carry = lax.fori_loop(0, total // UNROLL, group, (zero, zero, jnp.int32(-1)))
-    lax.fori_loop(total // UNROLL * UNROLL, total, place, carry)
-
-    depth = out_refs[0].shape[0]
-    for d, out_ref in enumerate(out_refs):
-        out_ref[...] = stage[d * depth : (d + 1) * depth, :].astype(jnp.bfloat16)
-
-
-def gram_kernel(scalar_ref, *refs):
-    x_refs, (out_ref, turn) = refs[:-2], refs[-2:]
-    sources = len(x_refs)
+    carry = (zero, zero, jnp.int32(-1))
+    groups = total // UNROLL
+    carry = lax.fori_loop(0, groups, lambda i, c: place(i * UNROLL, UNROLL, c), carry)
+    lax.fori_loop(groups * UNROLL, total, lambda i, c: place(i, 1, c), carry)
+
+    depth = out_ref.shape[1]
+    for d in range(out_ref.shape[0]):
+        out_ref[d] = stage[d * depth : (d + 1) * depth, :].astype(jnp.bfloat16)
+
+
+def gram_kernel(scalar_ref, x_ref, out_ref):
+    sources = x_ref.shape[0]
     frames = out_ref.shape[0]
     local = frames // sources
     pixels = scalar_ref[2]
-    tm_index = scalar_ref[4]
     lane = lax.broadcasted_iota(jnp.int32, (1, LANE), 1)
 
     def pair(j, carry):
         gram, total = carry
         rows = pl.ds(pl.multiple_of(j * 2 * local, 2 * local), 2 * local)
-        both = [ref[rows, :].astype(jnp.float32) for ref in x_refs]
+        both = [x_ref[source, rows, :].astype(jnp.float32) for source in range(sources)]
         exact, high, low = [], [], []
         for i in range(2):
             used = lane + (2 * j + i) * LANE < pixels
@@ -185,19 +192,11 @@
     def two_pairs(j, carry):
         return pair(2 * j + 1, pair(2 * j, carry))
 
-    def in_order(value):
-        for j in range(sources):
-            at = pl.multiple_of((tm_index ^ (sources - 1 - j)) * local, local)
-            turn[pl.ds(at, local), :] = value[j * local : (j + 1) * local]
-        return turn[...]
-
     carry = (jnp.zeros((frames, 2 * frames), jnp.float32), jnp.zeros((frames, LANE), jnp.float32))
     pairs = (pixels + 2 * LANE - 1) // (2 * LANE)
     carry = lax.fori_loop(0, pairs // 2, two_pairs, carry)
     gram, total = lax.fori_loop(pairs // 2 * 2, pairs, pair, carry)
-    gram = in_order(gram[:, :frames] + gram[:, frames:])
-    gram = in_order(gram.T)
-    total = in_order(total)
+    gram = gram[:, :frames] + gram[:, frames:]
     first = jnp.sum(total, axis=1, keepdims=True)
     second = jnp.sum(total.T, axis=0, keepdims=True)
     out_ref[...] = pixels.astype(jnp.float32) * gram / (first * second)
@@ -212,18 +211,23 @@
     params = pltpu.CompilerParams(vmem_limit_bytes=VMEM_LIMIT)
 
     far = lax.ppermute(frames, "tile", [(0, 1), (1, 0)])
-    where = jnp.stack([lax.axis_index("tm"), lax.axis_index("tile")]).astype(jnp.int32)
     words, scalars = pl.pallas_call(
         plan_kernel,
         out_shape=(
             jax.ShapeDtypeStruct((list_rows, LANE), jnp.int32),
-            jax.ShapeDtypeStruct((5,), jnp.int32),
+            jax.ShapeDtypeStruct((4,), jnp.int32),
         ),
-        in_specs=[smem, smem, vmem, vmem],
+        in_specs=[pl.BlockSpec(memory_space=pl.ANY)] * 3,
         out_specs=(vmem, smem),
+        scratch_shapes=[
+            pltpu.SMEM(cycle_owner.shape, jnp.int32),
+            pltpu.VMEM(block_cycle.shape, jnp.int32),
+            pltpu.VMEM(block_valid.shape, jnp.int32),
+            pltpu.SemaphoreType.DMA((3,)),
+        ],
         compiler_params=params,
         name="plan",
-    )(where, cycle_owner, block_cycle, block_valid)
+    )(cycle_owner, block_cycle, block_valid)
     words = words.reshape(-1)
 
     def branch(size):
@@ -232,9 +236,9 @@
         def run(words, scalars, near, far):
             send = pl.pallas_call(
                 pack_kernel,
-                out_shape=(jax.ShapeDtypeStruct((depth, LANE), jnp.bfloat16),) * tm_count,
+                out_shape=jax.ShapeDtypeStruct((tm_count, depth, LANE), jnp.bfloat16),
                 in_specs=[smem, smem, vmem, vmem],
-                out_specs=(vmem,) * tm_count,
+                out_specs=vmem,
                 scratch_shapes=[
                     pltpu.VMEM((local_frames * (2 * half + 1) + 8, LANE), jnp.float32),
                     pltpu.VMEM((tm_count * depth + local_frames, LANE), jnp.float32),
@@ -242,22 +246,17 @@
                 compiler_params=params,
                 name="pack",
             )(words, scalars, near, far)
-            got = []
-            for j in range(tm_count):
-                apart = tm_count - 1 - j
-                pairs = [(i, i ^ apart) for i in range(tm_count)]
-                got.append(lax.ppermute(send[j], "tm", pairs) if apart else send[j])
+            got = lax.all_to_all(send, "tm", split_axis=0, concat_axis=0, tiled=True)
             return pl.pallas_call(
                 gram_kernel,
                 out_shape=jax.ShapeDtypeStruct(
                     (tm_count * local_frames, tm_count * local_frames), jnp.float32
                 ),
-                in_specs=[smem] + [vmem] * tm_count,
+                in_specs=[smem, vmem],
                 out_specs=vmem,
-                scratch_shapes=[pltpu.VMEM((tm_count * local_frames, LANE), jnp.float32)],
                 compiler_params=params,
                 name="gram",
-            )(scalars, *got)
+            )(scalars, got)
 
         return run
 

time: 68.1 us -> 61.7 us (0.906)
  blocking collectives: 0 us -> 42.1 us
  starting transfers between devices: 35.4 us -> 0.45 us
  waiting for transfers between devices: 8.76 us -> 0.45 us
  Pallas kernels: 19.5 us -> 14.6 us
    all_to_all x0 -> x1, blocking collectives: none -> 42.1 us  [run(): got = lax.all_to_all(send, 'tm', split_axis=0, concat_axis=0, tiled=True)]
    ppermute x15 -> x0, starting transfers between devices: 35 us -> none  [run(): got.append(lax.ppermute(send[j], 'tm', pairs) if apart else send[j])]
    ppermute x15 -> x0, waiting for transfers between devices: 8.36 us -> none  [run(): got.append(lax.ppermute(send[j], 'tm', pairs) if apart else send[j])]
    pallas_call x1, Pallas kernels: 14.1 us -> 9.45 us  [run(): pl.pallas_call(pack_kernel, out_shape=jax.ShapeDtypeStruct((tm_count, dep...]
  transfers between devices with their start and end apart: 16 -> 1, of which waited for: 9 -> 1; matrix products, arithmetic and copies ran while one was open for 0% -> 0% of each run, Pallas kernels for 3% -> 3%
where the time goes in v3:
time: 61.7 us; the launch traced here: 60.6 us
  blocking collectives  42.1 us (68%)
  Pallas kernels  14.6 us (24%)
  local copies, waits for them, and re-layouts  2.69 us (4%)
    all_to_all x1, blocking collectives, run(): got = lax.all_to_all(send, 'tm', split_axis=0, concat_axis=0, tiled=True)  42.1 us
    pallas_call x1, Pallas kernels, run(): pl.pallas_call(pack_kernel, out_shape=jax.ShapeDtypeStruct((tm_count, dep...  9.45 us
    pallas_call x1, Pallas kernels, run(): pl.pallas_call(gram_kernel, out_shape=jax.ShapeDtypeStruct((tm_count * lo...  3.3 us
    unnamed x8, local copies, waits for them, and re-layouts  2.69 us
    pallas_call x1, Pallas kernels, on_device_routed(): pl.pallas_call(plan_kernel, out_shape=(jax.ShapeDtypeStruct((list_rows, L...  1.81 us
  transfers between devices with their start and end apart: 1, of which 1 were waited for; matrix products, arithmetic and copies ran while one was open for 0% of the time, Pallas kernels for 3%

profile of v3, /device:TPU:0, one launch (start us, length us, event | category | flops | bytes accessed | tf_op | source)
XLA Modules:
  0.0 60.6 jit_solution(2191435115372666817)
XLA Ops:
  0.0 0.5 collective-permute-start
  0.5 0.0 copy-start
  0.5 0.7 %copy-done = s32[2304]{0:T(1024)S(1)} copy-done((s32[2304]{0:T(1024)S(1)}, s32[2304]{0:T(1024)}, u32[]{:S(2)}) %copy-start) | copy-done | bytes 9240
  1.2 0.0 copy-start.1
  1.2 0.7 %copy-done.1 = s32[2304]{0:T(1024)S(1)} copy-done((s32[2304]{0:T(1024)S(1)}, s32[2304]{0:T(1024)}, u32[]{:S(2)}) %copy-start.1) | copy-done | bytes 9240
  1.9 0.0 copy-start.2
  1.9 0.7 %copy-done.2 = s32[32]{0:T(128)S(1)} copy-done((s32[32]{0:T(128)S(1)}, s32[32]{0:T(128)}, u32[]{:S(2)}) %copy-start.2) | copy-done | bytes 152
  2.5 1.8 %plan.1 = (s32[24,128]{1,0:T(8,128)S(1)}, s32[4]{0:T(128)S(1)}) custom-call(s32[32]{0:T(128)S(1)} %copy-done.2, s32[2304]{0:T(1024)S(1)} %copy-done, s32[2304]{0:T(1024)S(1)} %copy-done.1), custom_call_target="tpu_custom_call" | custom-call | tf_op jit(solution)/shard_map/plan/pallas_call | solution.py:214
  4.4 0.4 collective-permute-done
  4.8 55.1 %conditional.1 = (f32[128,128]{1,0:T(8,128)S(1)}) conditional(s32[]{:T(128)} %bitcast.15, (s32[24,128]{1,0:T(8,128)S(1)}, s32[4]{0:T(128)S(1)}, bf16[8,1152,128]{2,1,0:T(8,128)(2,1)}, bf16[8,1152,128]{2,1,0:T(8,128)(2,1)S(1)}) %tuple.50, (s32[24,128]{1,0:T(8,128)S(1)}, s32[4]{0:T(128)S(1)}, ...), branch_computations={%region_0.0_spmd, %region_1.0_spmd, %region_2.0_spmd, %region_3.0_... | conditional | bytes 9437192 | solution.py:263
  4.8 9.5 %pack.20 = bf16[16,336,128]{2,1,0:T(8,128)(2,1)S(1)} custom-call(s32[3072]{0:T(1024)S(1)} %bitcast.22, s32[4]{0:T(128)S(1)} %get-tuple-element.161.scalar_ref, bf16[8,1152,128]{2,1,0:T(8,128)(2,1)} %get-tuple-element.163.near_ref, bf16[8,1152,128]{2,1,0:T(8,128)(2,1)S(1)} %get-tuple-element.164.far_ref), custom_call_target="tpu_custom_call" | custom-call | tf_op jit(solution)/shard_map/cond/branch_5_fun/pack/pallas_call | solution.py:237
  14.3 42.1 %all_to_all.65.x_ref = bf16[16,336,128]{2,1,0:T(8,128)(2,1)S(1)} all-to-all(bf16[16,336,128]{2,1,0:T(8,128)(2,1)S(1)} %pack.20), channel_id=1, replica_groups=mesh['series'=1,'tm'=16,'tile'=2] {'tm'}, dimensions={0} | all-to-all | bytes 2752512 | tf_op jit(solution)/shard_map/cond/branch_5_fun/all_to_all | solution.py:249
  56.4 3.3 %gram.20 = f32[128,128]{1,0:T(8,128)S(1)} custom-call(s32[4]{0:T(128)S(1)} %get-tuple-element.161.scalar_ref, bf16[16,336,128]{2,1,0:T(8,128)(2,1)S(1)} %all_to_all.65.x_ref), custom_call_target="tpu_custom_call" | custom-call | tf_op jit(solution)/shard_map/cond/branch_5_fun/gram/pallas_call | solution.py:250
  60.0 0.0 copy-start.3
  60.0 0.6 %copy-done.3 = f32[128,128]{1,0:T(8,128)} copy-done((f32[128,128]{1,0:T(8,128)}, f32[128,128]{1,0:T(8,128)S(1)}, u32[]{:S(2)}) %copy-start.3) | copy-done | bytes 65560
Async XLA Ops:
  0.0 4.8 %collective-permute-start = (bf16[8,1152,128]{2,1,0:T(8,128)(2,1)}, bf16[8,1152,128]{2,1,0:T(8,128)(2,1)S(1)}, u32[]{:S(2)}, u32[]{:S(2)}) collective-permute-start(bf16[8,1152,128]{2,1,0:T(8,128)(2,1)} %param.19), channel_id=1, source_target_pairs={{0,1},{1,0},{2,3},{3,2},{4,5},{5,4},{6,7},{7,6},{8,9},{9,8},{10,11... | collective-permute-start | bytes 7077896 | tf_op jit(solution)/shard_map/ppermute | solution.py:213
  0.5 0.7 %copy-start = (s32[2304]{0:T(1024)S(1)}, s32[2304]{0:T(1024)}, u32[]{:S(2)}) copy-start(s32[2304]{0:T(1024)} %cycle_in.1) | copy-start | bytes 27652
  1.2 0.7 %copy-start.1 = (s32[2304]{0:T(1024)S(1)}, s32[2304]{0:T(1024)}, u32[]{:S(2)}) copy-start(s32[2304]{0:T(1024)} %valid_in.1) | copy-start | bytes 27652
  1.9 0.7 %copy-start.2 = (s32[32]{0:T(128)S(1)}, s32[32]{0:T(128)}, u32[]{:S(2)}) copy-start(s32[32]{0:T(128)} %owner_in.1) | copy-start | bytes 388
  60.0 0.6 %copy-start.3 = (f32[128,128]{1,0:T(8,128)}, f32[128,128]{1,0:T(8,128)S(1)}, u32[]{:S(2)}) copy-start(f32[128,128]{1,0:T(8,128)S(1)} %get-tuple-element.238) | copy-start | bytes 196612

commit v4 on v3

--- a/solution.py
+++ b/solution.py
@@ -102,17 +102,15 @@
         words = words + (lists[part * list_rows : (part + 1) * list_rows] << (8 * part))
     word_ref[...] = words
 
-    own_slot = 2 * tm_index + tile_index
     scalar_ref[0] = rung
     scalar_ref[1] = jnp.sum(count[:, :1] * mine[:, :1]).astype(jnp.int32)
-    scalar_ref[2] = jnp.sum(jnp.where(slot == own_slot, pixels, 0.0)[:, :1]).astype(jnp.int32)
-    scalar_ref[3] = tile_index
+    scalar_ref[2] = tile_index
 
 
 def pack_kernel(word_ref, scalar_ref, near_ref, far_ref, out_ref, pool, stage):
     frames, half, _ = near_ref.shape
     stride = 2 * half + 1
-    near_at = scalar_ref[3] * half
+    near_at = scalar_ref[2] * half
     far_at = half - near_at
     for source, at in ((near_ref, near_at), (far_ref, far_at)):
         for f in range(frames):
@@ -158,11 +156,11 @@
         out_ref[d] = stage[d * depth : (d + 1) * depth, :].astype(jnp.bfloat16)
 
 
-def gram_kernel(scalar_ref, x_ref, out_ref):
+def gram_kernel(pixel_ref, x_ref, out_ref):
     sources = x_ref.shape[0]
     frames = out_ref.shape[0]
     local = frames // sources
-    pixels = scalar_ref[2]
+    pixels = pixel_ref[0]
     lane = lax.broadcasted_iota(jnp.int32, (1, LANE), 1)
 
     def pair(j, carry):
@@ -215,9 +213,9 @@
         plan_kernel,
         out_shape=(
             jax.ShapeDtypeStruct((list_rows, LANE), jnp.int32),
-            jax.ShapeDtypeStruct((4,), jnp.int32),
+            jax.ShapeDtypeStruct((3,), jnp.int32),
         ),
-        in_specs=[pl.BlockSpec(memory_space=pl.ANY)] * 3,
+        in_specs=[pl.BlockSpec(memory_space=pltpu.HBM)] * 3,
         out_specs=(vmem, smem),
         scratch_shapes=[
             pltpu.SMEM(cycle_owner.shape, jnp.int32),
@@ -233,7 +231,7 @@
     def branch(size):
         depth = size * local_frames
 
-        def run(words, scalars, near, far):
+        def run(words, scalars, near, far, block_cycle, block_valid, cycle_owner):
             send = pl.pallas_call(
                 pack_kernel,
                 out_shape=jax.ShapeDtypeStruct((tm_count, depth, LANE), jnp.bfloat16),
@@ -246,6 +244,8 @@
                 compiler_params=params,
                 name="pack",
             )(words, scalars, near, far)
+            own = cycle_owner[2 * lax.axis_index("tm") + lax.axis_index("tile")]
+            pixels = jnp.sum(jnp.where(block_cycle == own, block_valid, 0), keepdims=True)
             got = lax.all_to_all(send, "tm", split_axis=0, concat_axis=0, tiled=True)
             return pl.pallas_call(
                 gram_kernel,
@@ -256,12 +256,20 @@
                 out_specs=vmem,
                 compiler_params=params,
                 name="gram",
-            )(scalars, got)
+            )(pixels, got)
 
         return run
 
     return lax.switch(
-        scalars[0], [branch(size) for size in LADDER], words, scalars, frames, far
+        scalars[0],
+        [branch(size) for size in LADDER],
+        words,
+        scalars,
+        frames,
+        far,
+        block_cycle,
+        block_valid,
+        cycle_owner,
     )
 
 

time: 61.7 us -> 60.7 us (0.984)
  blocking collectives: 42.1 us -> 0 us
  waiting for transfers between devices: 0.45 us -> 32.4 us
  starting transfers between devices: 0.45 us -> 8.83 us
  Pallas kernels: 14.6 us -> 16.9 us
  local copies, waits for them, and re-layouts: 2.69 us -> 0.6 us
  other arithmetic: 0 us -> 1.27 us
    all_to_all x1 -> x0, blocking collectives: 42.1 us -> none  [run(): got = lax.all_to_all(send, 'tm', split_axis=0, concat_axis=0, tiled=True)]
    all_to_all x0 -> x1, waiting for transfers between devices: none -> 30.1 us  [run(): got = lax.all_to_all(send, 'tm', split_axis=0, concat_axis=0, tiled=True)]
    all_to_all x0 -> x1, starting transfers between devices: none -> 8.37 us  [run(): got = lax.all_to_all(send, 'tm', split_axis=0, concat_axis=0, tiled=True)]
    unnamed x8 -> x0, local copies, waits for them, and re-layouts: 2.69 us -> none
    ppermute x1, waiting for transfers between devices: 0.45 us -> 2.34 us  [on_device_routed(): far = lax.ppermute(frames, 'tile', [(0, 1), (1, 0)])]
    reduce_sum x0 -> x1, other arithmetic: none -> 1.27 us  [run(): jnp.sum(jnp.where(block_cycle == own, block_valid, 0), keepdims=True)]
    pallas_call x1, Pallas kernels: 9.45 us -> 10.6 us  [run(): pl.pallas_call(pack_kernel, out_shape=jax.ShapeDtypeStruct((tm_count, dep...]
    pallas_call x1, Pallas kernels: 3.3 us -> 4.26 us  [run(): pl.pallas_call(gram_kernel, out_shape=jax.ShapeDtypeStruct((tm_count * lo...]
  transfers between devices with their start and end apart: 1 -> 2, of which waited for: 1 -> 2; matrix products, arithmetic and copies ran while one was open for 0% -> 3% of each run, Pallas kernels for 3% -> 3%
where the time goes in v4:
time: 60.7 us; the launch traced here: 60 us
  waiting for transfers between devices  32.4 us (53%)
  Pallas kernels  16.9 us (28%)
  starting transfers between devices  8.83 us (15%)
  other arithmetic  1.27 us (2%)
    all_to_all x1, waiting for transfers between devices, run(): got = lax.all_to_all(send, 'tm', split_axis=0, concat_axis=0, tiled=True)  30.1 us
    pallas_call x1, Pallas kernels, run(): pl.pallas_call(pack_kernel, out_shape=jax.ShapeDtypeStruct((tm_count, dep...  10.6 us
    all_to_all x1, starting transfers between devices, run(): got = lax.all_to_all(send, 'tm', split_axis=0, concat_axis=0, tiled=True)  8.37 us
    pallas_call x1, Pallas kernels, run(): pl.pallas_call(gram_kernel, out_shape=jax.ShapeDtypeStruct((tm_count * lo...  4.26 us
    ppermute x1, waiting for transfers between devices, on_device_routed(): far = lax.ppermute(frames, 'tile', [(0, 1), (1, 0)])  2.34 us
    pallas_call x1, Pallas kernels, on_device_routed(): pl.pallas_call(plan_kernel, out_shape=(jax.ShapeDtypeStruct((list_rows, L...  1.98 us
    reduce_sum x1, other arithmetic, run(): jnp.sum(jnp.where(block_cycle == own, block_valid, 0), keepdims=True)  1.27 us
  transfers between devices with their start and end apart: 2, of which 2 were waited for; matrix products, arithmetic and copies ran while one was open for 3% of the time, Pallas kernels for 3%

profile of v4, /device:TPU:0, one launch (start us, length us, event | category | flops | bytes accessed | tf_op | source)
XLA Modules:
  0.0 60.0 jit_solution(10228917718016527000)
XLA Ops:
  0.0 0.5 collective-permute-start
  0.5 2.0 %plan.1 = (s32[24,128]{1,0:T(8,128)S(1)}, s32[3]{0:T(128)S(1)}) custom-call(s32[32]{0:T(128)} %owner_in.1, s32[2304]{0:T(1024)} %cycle_in.1, s32[2304]{0:T(1024)} %valid_in.1), custom_call_target="tpu_custom_call" | custom-call | tf_op jit(solution)/shard_map/plan/pallas_call | solution.py:212
  2.5 2.3 %collective-permute-done = bf16[8,1152,128]{2,1,0:T(8,128)(2,1)S(1)} collective-permute-done((bf16[8,1152,128]{2,1,0:T(8,128)(2,1)}, bf16[8,1152,128]{2,1,0:T(8,128)(2,1)S(1)}, u32[]{:S(2)}, u32[]{:S(2)}) %collective-permute-start) | collective-permute-done | bytes 2359328 | tf_op jit(solution)/shard_map/ppermute | solution.py:211
  4.8 55.2 %conditional.1 = (f32[128,128]{1,0:T(8,128)}) conditional(s32[]{:T(128)} %bitcast.45, (s32[32]{0:T(128)}, s32[2304]{0:T(1024)}, s32[2304]{0:T(1024)}, s32[24,128]{1,0:T(8,128)S(1)}, s32[3]{0:T(128)S(1)}, /*index=5*/bf16[8,1152,128]{2,1,0:T(8,128)(2,1)}, bf16[8,1152,128]{2,1,0:T(8,128)(2,1)S(1)}) %tuple.50, ...), branch_computations={%region_0.2_spmd, %region_2.4_spmd, %region_4.6_spmd, %region_6.8_... | conditional | flops 6921 | bytes 33123098 | solution.py:263
  4.8 10.6 %pack.21 = bf16[16,352,128]{2,1,0:T(8,128)(2,1)} custom-call(s32[3072]{0:T(1024)S(1)} %bitcast.53, s32[3]{0:T(128)S(1)} %get-tuple-element.277.scalar_ref, bf16[8,1152,128]{2,1,0:T(8,128)(2,1)} %get-tuple-element.278.near_ref, bf16[8,1152,128]{2,1,0:T(8,128)(2,1)S(1)} %get-tuple-element.279.far_ref), custom_call_target="tpu_custom_call" | custom-call | tf_op jit(solution)/shard_map/cond/branch_6_fun/pack/pallas_call | solution.py:235
  15.4 0.0 copy-start.40
  15.5 0.0 copy-start.10
  15.5 0.0 copy-start.25
  15.5 8.4 %all-to-all-start.6 = ((bf16[16,352,128]{2,1,0:T(8,128)(2,1)}), bf16[16,352,128]{2,1,0:T(8,128)(2,1)S(1)}, u32[]{:S(2)}, u32[]{:S(2)}) async-start(bf16[16,352,128]{2,1,0:T(8,128)(2,1)} %pack.21), calls=%async_computation.6 | async-start | bytes 2883584 | tf_op jit(solution)/shard_map/cond/branch_6_fun/all_to_all | solution.py:249
  23.8 0.0 copy-done.40
  23.9 0.6 dynamic_slice.36
  24.4 0.0 copy-done.10
  24.4 0.0 copy-done.25
  24.4 1.3 %select_reduce_fusion.6 = s32[]{:T(128)} fusion(s32[2304]{0:T(1024)S(1)} %copy-done.25, s32[2304]{0:T(1024)S(1)} %copy-done.10, s32[]{:T(128)} %bitcast.18), kind=kLoop, calls=%fused_computation.6 | loop fusion | flops 6911 | bytes 18440 | tf_op jit(solution)/shard_map/cond/branch_6_fun/reduce_sum | solution.py:248
  25.7 30.1 %all-to-all-done.6.x_ref = bf16[16,352,128]{2,1,0:T(8,128)(2,1)S(1)} async-done(((bf16[16,352,128]{2,1,0:T(8,128)(2,1)}), bf16[16,352,128]{2,1,0:T(8,128)(2,1)S(1)}, u32[]{:S(2)}, u32[]{:S(2)}) %all-to-all-start.6) | async-done | bytes 1441824 | tf_op jit(solution)/shard_map/cond/branch_6_fun/all_to_all | solution.py:249
  55.8 4.3 %gram.21 = f32[128,128]{1,0:T(8,128)} custom-call(s32[1]{0:T(128)} %bitcast.19.pixel_ref, bf16[16,352,128]{2,1,0:T(8,128)(2,1)S(1)} %all-to-all-done.6.x_ref), custom_call_target="tpu_custom_call" | custom-call | tf_op jit(solution)/shard_map/cond/branch_6_fun/gram/pallas_call | solution.py:250
Async XLA Ops:
  0.0 4.8 %collective-permute-start = (bf16[8,1152,128]{2,1,0:T(8,128)(2,1)}, bf16[8,1152,128]{2,1,0:T(8,128)(2,1)S(1)}, u32[]{:S(2)}, u32[]{:S(2)}) collective-permute-start(bf16[8,1152,128]{2,1,0:T(8,128)(2,1)} %param.19), channel_id=1, source_target_pairs={{0,1},{1,0},{2,3},{3,2},{4,5},{5,4},{6,7},{7,6},{8,9},{9,8},{10,11... | collective-permute-start | bytes 7077896 | tf_op jit(solution)/shard_map/ppermute | solution.py:211
  15.4 8.4 %copy-start.40 = (s32[32]{0:T(128)S(1)}, s32[32]{0:T(128)}, u32[]{:S(2)}) copy-start(s32[32]{0:T(128)} %get-tuple-element.274) | copy-start | bytes 388 | tf_op jit(solution)/shard_map/cond
  15.5 9.0 %copy-start.10 = (s32[2304]{0:T(1024)S(1)}, s32[2304]{0:T(1024)}, u32[]{:S(2)}) copy-start(s32[2304]{0:T(1024)} %get-tuple-element.273) | copy-start | bytes 27652 | tf_op jit(solution)/shard_map/cond
  15.5 9.0 %copy-start.25 = (s32[2304]{0:T(1024)S(1)}, s32[2304]{0:T(1024)}, u32[]{:S(2)}) copy-start(s32[2304]{0:T(1024)} %get-tuple-element.275) | copy-start | bytes 27652 | tf_op jit(solution)/shard_map/cond
  15.5 40.3 %all-to-all-start.6 = ((bf16[16,352,128]{2,1,0:T(8,128)(2,1)}), bf16[16,352,128]{2,1,0:T(8,128)(2,1)S(1)}, u32[]{:S(2)}, u32[]{:S(2)}) async-start(bf16[16,352,128]{2,1,0:T(8,128)(2,1)} %pack.21), calls=%async_computation.6 | async-start | bytes 2883584 | tf_op jit(solution)/shard_map/cond/branch_6_fun/all_to_all | solution.py:249

commit v5 on v3

--- a/solution.py
+++ b/solution.py
@@ -9,10 +9,16 @@
 
 LANE = 128
 UNROLL = 16
+GROUPS = 2
 STEP = 384
-VMEM_LIMIT = 48 * 1024 * 1024
+VMEM_LIMIT = 24 * 1024 * 1024
 LADDER = (16, 24, 32, 36, 40, 42, 44, 46, 48, 52, 56, 64, 80, 104, 144)
 NT = (((1,), (1,)), ((), ()))
+
+
+def apart_of(turn, count):
+    side = count // 2
+    return (side if turn % 2 == 0 else 0) + side - 1 - turn // 2
 
 
 def plan_kernel(
@@ -31,6 +37,7 @@
         fetch.wait()
     chunks = cycle_ref.shape[0] // LANE
     slots = owner_ref.shape[0]
+    half = cycle_ref.shape[0] // 2
     list_rows = word_ref.shape[0]
     slot = lax.broadcasted_iota(jnp.int32, (slots, LANE), 0)
     mine = (slot % 2 == tile_index).astype(jnp.float32)
@@ -68,13 +75,19 @@
         rung = rung + (rows > smaller).astype(jnp.int32)
         size = jnp.where(rows > smaller, larger, size)
 
-    row = lax.broadcasted_iota(jnp.int32, (slots, slots), 0)
-    col = lax.broadcasted_iota(jnp.int32, (slots, slots), 1)
-    earlier = ((col < row) & (col % 2 == tile_index)).astype(jnp.float32)
+    def turn_of(index):
+        apart = (index // 2) ^ tm_index
+        side = slots // 4
+        return 2 * (side - 1 - apart % side) + (apart < side).astype(jnp.int32)
+
+    row = turn_of(lax.broadcasted_iota(jnp.int32, (slots, slots), 0))
+    index = lax.broadcasted_iota(jnp.int32, (slots, slots), 1)
+    earlier = ((turn_of(index) < row) & (index % 2 == tile_index)).astype(jnp.float32)
+    turn = turn_of(slot)
     base = jnp.dot(
         earlier, count, precision=lax.Precision.HIGHEST, preferred_element_type=jnp.float32
     )
-    begin = (slot // 2 * size * LANE).astype(jnp.float32)
+    begin = (turn * size * LANE).astype(jnp.float32)
 
     list_row = lax.broadcasted_iota(jnp.int32, (list_rows, LANE), 0)
     list_col = lax.broadcasted_iota(jnp.int32, (LANE, LANE), 0)
@@ -85,7 +98,10 @@
         place = jnp.sum(own * (rank[k] + base), axis=0, keepdims=True).astype(jnp.int32)
         at = jnp.sum(own * (start[k] + begin), axis=0, keepdims=True).astype(jnp.int32)
         used = jnp.sum(own, axis=0, keepdims=True) > 0
-        word = at * 4096 + (k * LANE + lane)
+        block = k * LANE + lane
+        far = (block >= half) != (tile_index == 1)
+        block = jnp.where(block >= half, block - half, block) + jnp.where(far, 2048, 0)
+        word = at * 4096 + block
         at_row = list_row == jnp.where(used, place // LANE, -1)
         at_col = (list_col == place % LANE).astype(jnp.float32).astype(jnp.bfloat16)
         spread = jnp.concatenate(
@@ -104,27 +120,32 @@
 
     own_slot = 2 * tm_index + tile_index
     scalar_ref[0] = rung
-    scalar_ref[1] = jnp.sum(count[:, :1] * mine[:, :1]).astype(jnp.int32)
+    scalar_ref[1] = tm_index
     scalar_ref[2] = jnp.sum(jnp.where(slot == own_slot, pixels, 0.0)[:, :1]).astype(jnp.int32)
-    scalar_ref[3] = tile_index
-
-
-def pack_kernel(word_ref, scalar_ref, near_ref, far_ref, out_ref, pool, stage):
-    frames, half, _ = near_ref.shape
-    stride = 2 * half + 1
-    near_at = scalar_ref[3] * half
-    far_at = half - near_at
-    for source, at in ((near_ref, near_at), (far_ref, far_at)):
-        for f in range(frames):
-
-            def widen(i, _, source=source, at=at, f=f):
-                begin = pl.multiple_of(i * STEP, STEP)
-                to = f * stride + pl.multiple_of(at + begin, 8)
-                pool[pl.ds(to, STEP), :] = source[f, pl.ds(begin, STEP), :].astype(jnp.float32)
-                return 0
-
-            lax.fori_loop(0, half // STEP, widen, 0)
-
+    for group in range(GROUPS + 1):
+        ahead = jnp.where(turn * GROUPS < group * (slots // 2), count * mine, 0.0)
+        scalar_ref[3 + group] = jnp.sum(ahead[:, :1]).astype(jnp.int32)
+
+
+def widen_kernel(in_ref, out_ref):
+    frames, half, _ = in_ref.shape
+    for f in range(frames):
+
+        def widen(i, _, f=f):
+            begin = pl.multiple_of(i * STEP, STEP)
+            rows = in_ref[f, pl.ds(begin, STEP), :].astype(jnp.float32)
+            out_ref[pl.ds(f * (half + 1) + begin, STEP), :] = rows
+            return 0
+
+        lax.fori_loop(0, half // STEP, widen, 0)
+
+
+def pack_kernel(group, word_ref, scalar_ref, near_ref, far_ref, *rest):
+    out_refs, stage = rest[:-1], rest[-1]
+    depth = out_refs[0].shape[0]
+    frames = 8
+    stride = near_ref.shape[0] // frames
+    first_row = group * len(out_refs) * (depth // frames)
     lane = lax.broadcasted_iota(jnp.int32, (frames, LANE), 1)
 
     def place(i, count, carry):
@@ -132,8 +153,9 @@
         turned, row, shift = [], [], []
         for j in range(count):
             word = word_ref[i + j]
-            x = pool[pl.ds(word & 4095, frames, stride=stride), :]
-            row.append(word >> 19)
+            at = pl.ds(word & 2047, frames, stride=stride)
+            x = jnp.where((word & 2048) == 0, near_ref[at, :], far_ref[at, :])
+            row.append((word >> 19) - first_row)
             shift.append((word >> 12) & (LANE - 1))
             turned.append(pltpu.roll(x, shift[j], 1))
         for j in range(count):
@@ -146,29 +168,29 @@
             stage[pl.ds(at + frames, frames), :] = spill
         return held, spill, last
 
-    total = scalar_ref[1]
+    begin, end = scalar_ref[3 + group], scalar_ref[4 + group]
     zero = jnp.zeros((frames, LANE), jnp.float32)
     carry = (zero, zero, jnp.int32(-1))
-    groups = total // UNROLL
-    carry = lax.fori_loop(0, groups, lambda i, c: place(i * UNROLL, UNROLL, c), carry)
-    lax.fori_loop(groups * UNROLL, total, lambda i, c: place(i, 1, c), carry)
-
-    depth = out_ref.shape[1]
-    for d in range(out_ref.shape[0]):
-        out_ref[d] = stage[d * depth : (d + 1) * depth, :].astype(jnp.bfloat16)
-
-
-def gram_kernel(scalar_ref, x_ref, out_ref):
-    sources = x_ref.shape[0]
+    groups = (end - begin) // UNROLL
+    carry = lax.fori_loop(0, groups, lambda i, c: place(begin + i * UNROLL, UNROLL, c), carry)
+    lax.fori_loop(begin + groups * UNROLL, end, lambda i, c: place(i, 1, c), carry)
+    for d, out_ref in enumerate(out_refs):
+        out_ref[...] = stage[d * depth : (d + 1) * depth, :].astype(jnp.bfloat16)
+
+
+def gram_kernel(scalar_ref, *refs):
+    x_refs, (out_ref, turn) = refs[:-2], refs[-2:]
+    sources = len(x_refs)
     frames = out_ref.shape[0]
     local = frames // sources
     pixels = scalar_ref[2]
+    tm_index = scalar_ref[1]
     lane = lax.broadcasted_iota(jnp.int32, (1, LANE), 1)
 
     def pair(j, carry):
         gram, total = carry
         rows = pl.ds(pl.multiple_of(j * 2 * local, 2 * local), 2 * local)
-        both = [x_ref[source, rows, :].astype(jnp.float32) for source in range(sources)]
+        both = [ref[rows, :].astype(jnp.float32) for ref in x_refs]
         exact, high, low = [], [], []
         for i in range(2):
             used = lane + (2 * j + i) * LANE < pixels
@@ -192,11 +214,19 @@
     def two_pairs(j, carry):
         return pair(2 * j + 1, pair(2 * j, carry))
 
+    def in_order(value):
+        for j in range(sources):
+            at = pl.multiple_of((tm_index ^ apart_of(j, sources)) * local, local)
+            turn[pl.ds(at, local), :] = value[j * local : (j + 1) * local]
+        return turn[...]
+
     carry = (jnp.zeros((frames, 2 * frames), jnp.float32), jnp.zeros((frames, LANE), jnp.float32))
     pairs = (pixels + 2 * LANE - 1) // (2 * LANE)
     carry = lax.fori_loop(0, pairs // 2, two_pairs, carry)
     gram, total = lax.fori_loop(pairs // 2 * 2, pairs, pair, carry)
-    gram = gram[:, :frames] + gram[:, frames:]
+    gram = in_order(gram[:, :frames] + gram[:, frames:])
+    gram = in_order(gram.T)
+    total = in_order(total)
     first = jnp.sum(total, axis=1, keepdims=True)
     second = jnp.sum(total.T, axis=0, keepdims=True)
     out_ref[...] = pixels.astype(jnp.float32) * gram / (first * second)
@@ -205,19 +235,30 @@
 def on_device_routed(frames, block_cycle, block_valid, cycle_owner):
     tm_count = lax.axis_size("tm")
     local_frames, half, _ = frames.shape
+    frame_count = tm_count * local_frames
     list_rows = -(-block_cycle.shape[0] // (8 * LANE)) * 8
     vmem = pl.BlockSpec(memory_space=pltpu.VMEM)
     smem = pl.BlockSpec(memory_space=pltpu.SMEM)
     params = pltpu.CompilerParams(vmem_limit_bytes=VMEM_LIMIT)
+
+    def widen(part):
+        return pl.pallas_call(
+            widen_kernel,
+            out_shape=jax.ShapeDtypeStruct((local_frames * (half + 1), LANE), jnp.float32),
+            in_specs=[vmem],
+            out_specs=vmem,
+            compiler_params=params,
+            name="widen",
+        )(part)
 
     far = lax.ppermute(frames, "tile", [(0, 1), (1, 0)])
     words, scalars = pl.pallas_call(
         plan_kernel,
         out_shape=(
             jax.ShapeDtypeStruct((list_rows, LANE), jnp.int32),
-            jax.ShapeDtypeStruct((4,), jnp.int32),
+            jax.ShapeDtypeStruct((4 + GROUPS,), jnp.int32),
         ),
-        in_specs=[pl.BlockSpec(memory_space=pl.ANY)] * 3,
+        in_specs=[pl.BlockSpec(memory_space=pltpu.HBM)] * 3,
         out_specs=(vmem, smem),
         scratch_shapes=[
             pltpu.SMEM(cycle_owner.shape, jnp.int32),
@@ -228,40 +269,51 @@
         compiler_params=params,
         name="plan",
     )(cycle_owner, block_cycle, block_valid)
-    words = words.reshape(-1)
+    near_pool = widen(frames)
+    far_pool = widen(far)
+    members = tm_count // GROUPS
 
     def branch(size):
         depth = size * local_frames
 
-        def run(words, scalars, near, far):
-            send = pl.pallas_call(
-                pack_kernel,
-                out_shape=jax.ShapeDtypeStruct((tm_count, depth, LANE), jnp.bfloat16),
-                in_specs=[smem, smem, vmem, vmem],
-                out_specs=vmem,
-                scratch_shapes=[
-                    pltpu.VMEM((local_frames * (2 * half + 1) + 8, LANE), jnp.float32),
-                    pltpu.VMEM((tm_count * depth + local_frames, LANE), jnp.float32),
-                ],
-                compiler_params=params,
-                name="pack",
-            )(words, scalars, near, far)
-            got = lax.all_to_all(send, "tm", split_axis=0, concat_axis=0, tiled=True)
+        def run(words, scalars, near_pool, far_pool):
+            got = []
+            for group in range(GROUPS):
+                send = pl.pallas_call(
+                    functools.partial(pack_kernel, group),
+                    out_shape=(jax.ShapeDtypeStruct((depth, LANE), jnp.bfloat16),) * members,
+                    in_specs=[smem, smem, vmem, vmem],
+                    out_specs=(vmem,) * members,
+                    scratch_shapes=[pltpu.VMEM((members * depth + local_frames, LANE), jnp.float32)],
+                    compiler_params=params,
+                    cost_estimate=pl.CostEstimate(
+                        flops=2_000_000, bytes_accessed=16_000_000, transcendentals=0
+                    ),
+                    name="pack",
+                )(words, scalars, near_pool, far_pool)
+                for j in range(members):
+                    apart = apart_of(group * members + j, tm_count)
+                    pairs = [(i, i ^ apart) for i in range(tm_count)]
+                    got.append(lax.ppermute(send[j], "tm", pairs) if apart else send[j])
             return pl.pallas_call(
                 gram_kernel,
-                out_shape=jax.ShapeDtypeStruct(
-                    (tm_count * local_frames, tm_count * local_frames), jnp.float32
-                ),
-                in_specs=[smem, vmem],
+                out_shape=jax.ShapeDtypeStruct((frame_count, frame_count), jnp.float32),
+                in_specs=[smem] + [vmem] * tm_count,
                 out_specs=vmem,
+                scratch_shapes=[pltpu.VMEM((frame_count, LANE), jnp.float32)],
                 compiler_params=params,
                 name="gram",
-            )(scalars, got)
+            )(scalars, *got)
 
         return run
 
     return lax.switch(
-        scalars[0], [branch(size) for size in LADDER], words, scalars, frames, far
+        scalars[0],
+        [branch(size) for size in LADDER],
+        words.reshape(-1),
+        scalars,
+        near_pool,
+        far_pool,
     )
 
 

time: 61.7 us -> 54.5 us (0.88); the launches traced: 60.6 us -> 54.3 us
  blocking collectives: 42.1 us -> 0 us
  starting transfers between devices: 0.45 us -> 29.6 us
  waiting for transfers between devices: 0.45 us -> 5.19 us
  Pallas kernels: 14.6 us -> 16 us
    all_to_all x1 -> x0, blocking collectives: 42.1 us -> none  [run(): got = lax.all_to_all(send, 'tm', split_axis=0, concat_axis=0, tiled=True)]
    ppermute x0 -> x15, starting transfers between devices: none -> 29.2 us  [run(): got.append(lax.ppermute(send[j], 'tm', pairs) if apart else send[j])]
    ppermute x0 -> x15, waiting for transfers between devices: none -> 5.07 us  [run(): got.append(lax.ppermute(send[j], 'tm', pairs) if apart else send[j])]
    pallas_call x2 -> x5, Pallas kernels: 12.8 us -> 14.2 us  [the longest x2 9.83 us: run(): pl.pallas_call(functools.partial(pack_kernel, group), out_shape=(jax.Shap...]
    unnamed x8 -> x10, local copies, waits for them, and re-layouts: 2.69 us -> 2.61 us
  transfers between devices with their start and end apart: 1 -> 16, of which waited for: 1 -> 4; matrix products, arithmetic and copies ran while one was open for 0% -> 0% of each run, Pallas kernels for 3% -> 13%
where the time goes in v5:
time: 54.5 us; the launch traced here: 54.3 us
  starting transfers between devices  29.6 us (54%)
  Pallas kernels  16 us (29%)
  waiting for transfers between devices  5.19 us (10%)
  local copies, waits for them, and re-layouts  2.61 us (5%)
  loops' own time  0.79 us (1%)
    ppermute x15, starting transfers between devices, run(): got.append(lax.ppermute(send[j], 'tm', pairs) if apart else send[j])  29.2 us
    pallas_call x2, Pallas kernels, run(): pl.pallas_call(functools.partial(pack_kernel, group), out_shape=(jax.Shap...  9.83 us
    ppermute x15, waiting for transfers between devices, run(): got.append(lax.ppermute(send[j], 'tm', pairs) if apart else send[j])  5.07 us
    pallas_call x1, Pallas kernels, run(): pl.pallas_call(gram_kernel, out_shape=jax.ShapeDtypeStruct((frame_count,...  3.54 us
    unnamed x10, local copies, waits for them, and re-layouts  2.61 us
    pallas_call x1, Pallas kernels, on_device_routed(): pl.pallas_call(plan_kernel, out_shape=(jax.ShapeDtypeStruct((list_rows, L...  1.82 us
  transfers between devices with their start and end apart: 16, of which 4 were waited for; matrix products, arithmetic and copies ran while one was open for 0% of the time, Pallas kernels for 13%

profile of v5, /device:TPU:0, one launch (start us, length us, event | category | flops | bytes accessed | tf_op | source)
XLA Modules:
  0.0 54.3 jit_solution(14386287712278557875)
XLA Ops:
  0.0 0.5 collective-permute-start.225
  0.5 1.7 %copy-done = bf16[8,1152,128]{2,1,0:T(8,128)(2,1)S(1)} copy-done((bf16[8,1152,128]{2,1,0:T(8,128)(2,1)S(1)}, bf16[8,1152,128]{2,1,0:T(8,128)(2,1)}, u32[]{:S(2)}) %copy-start) | copy-done | bytes 2359320
  2.1 0.4 widen.2
  2.5 0.3 copy-done.1
  2.8 0.0 copy-done.2
  2.8 1.8 %plan.1 = (s32[24,128]{1,0:T(8,128)S(1)}, s32[6]{0:T(128)S(1)}) custom-call(s32[32]{0:T(128)S(1)} %copy-done.3, s32[2304]{0:T(1024)S(1)} %copy-done.1, s32[2304]{0:T(1024)S(1)} %copy-done.2), custom_call_target="tpu_custom_call" | custom-call | tf_op jit(solution)/shard_map/plan/pallas_call | solution.py:255
  4.7 0.1 collective-permute-done.225.in_ref
  4.8 0.4 widen.3
  5.2 48.4 %conditional.1 = (f32[128,128]{1,0:T(8,128)S(1)}) conditional(s32[]{:T(128)} %bitcast.15, (s32[24,128]{1,0:T(8,128)S(1)}, s32[6]{0:T(128)S(1)}, f32[9224,128]{1,0:T(8,128)S(1)}, f32[9224,128]{1,0:T(8,128)S(1)}) %tuple.50, (s32[24,128]{1,0:T(8,128)S(1)}, s32[6]{0:T(128)S(1)}, f32[9224,128]{1,0:T(8,128)S(1)}, ...), branch_computations={%region_0.0_spmd, %region_1.0_spmd, %region_2.0_spmd, %region_3.0_... | conditional | flops 4000000 | bytes 49695328 | solution.py:310
  5.5 4.9 %pack.41 = (bf16[336,128]{1,0:T(8,128)(2,1)S(1)}, bf16[336,128]{1,0:T(8,128)(2,1)S(1)}, bf16[336,128]{1,0:T(8,128)(2,1)S(1)}, bf16[336,128]{1,0:T(8,128)(2,1)S(1...) custom-call(s32[3072]{0:T(1024)S(1)} %bitcast.27, ...), custom_call_target="tpu_custom_call" | custom-call | flops 2000000 | bytes 16000000 | tf_op jit(solution)/shard_map/cond/branch_5_fun/pack/pallas_call | solution.py:282
  10.4 5.9 %collective-permute-start.83 = (bf16[336,128]{1,0:T(8,128)(2,1)S(1)}, bf16[336,128]{1,0:T(8,128)(2,1)S(1)}, u32[]{:S(2)}, u32[]{:S(2)}) collective-permute-start(bf16[336,128]{1,0:T(8,128)(2,1)S(1)} %get-tuple-element.253), channel_id=1, source_target_pairs={{0,22},{2,20},{4,18},{6,16},{8,30},{10,28},{12,26},{14,24},{16,6},... | collective-permute-start | bytes 258056 | tf_op jit(solution)/shard_map/cond/branch_5_fun/ppermute | solution.py:297
  16.3 0.5 collective-permute-start.84
  16.8 1.3 %collective-permute-start.85 = (bf16[336,128]{1,0:T(8,128)(2,1)S(1)}, bf16[336,128]{1,0:T(8,128)(2,1)S(1)}, u32[]{:S(2)}, u32[]{:S(2)}) collective-permute-start(bf16[336,128]{1,0:T(8,128)(2,1)S(1)} %get-tuple-element.255), channel_id=1, source_target_pairs={{0,20},{2,22},{4,16},{6,18},{8,28},{10,30},{12,24},{14,26},{16,4},... | collective-permute-start | bytes 258056 | tf_op jit(solution)/shard_map/cond/branch_5_fun/ppermute | solution.py:297
  18.1 0.3 collective-permute-start.86
  18.4 3.7 %collective-permute-start.87 = (bf16[336,128]{1,0:T(8,128)(2,1)S(1)}, bf16[336,128]{1,0:T(8,128)(2,1)S(1)}, u32[]{:S(2)}, u32[]{:S(2)}) collective-permute-start(bf16[336,128]{1,0:T(8,128)(2,1)S(1)} %get-tuple-element.257), channel_id=1, source_target_pairs={{0,18},{2,16},{4,22},{6,20},{8,26},{10,24},{12,30},{14,28},{16,2},... | collective-permute-start | bytes 258056 | tf_op jit(solution)/shard_map/cond/branch_5_fun/ppermute | solution.py:297
  22.1 4.9 %pack.40 = (bf16[336,128]{1,0:T(8,128)(2,1)S(1)}, bf16[336,128]{1,0:T(8,128)(2,1)S(1)}, bf16[336,128]{1,0:T(8,128)(2,1)S(1)}, bf16[336,128]{1,0:T(8,128)(2,1)S(1...) custom-call(s32[3072]{0:T(1024)S(1)} %bitcast.28, ...), custom_call_target="tpu_custom_call" | custom-call | flops 2000000 | bytes 16000000 | tf_op jit(solution)/shard_map/cond/branch_5_fun/pack/pallas_call | solution.py:282
  27.0 0.6 %collective-permute-start.88 = (bf16[336,128]{1,0:T(8,128)(2,1)S(1)}, bf16[336,128]{1,0:T(8,128)(2,1)S(1)}, u32[]{:S(2)}, u32[]{:S(2)}) collective-permute-start(bf16[336,128]{1,0:T(8,128)(2,1)S(1)} %get-tuple-element.258), channel_id=1, source_target_pairs={{0,2},{2,0},{4,6},{6,4},{8,10},{10,8},{12,14},{14,12},{16,18},{18,... | collective-permute-start | bytes 258056 | tf_op jit(solution)/shard_map/cond/branch_5_fun/ppermute | solution.py:297
  27.6 0.2 collective-permute-start.89
  27.8 0.0 collective-permute-done.85.refs_10_
  27.8 5.7 %collective-permute-start.75 = (bf16[336,128]{1,0:T(8,128)(2,1)S(1)}, bf16[336,128]{1,0:T(8,128)(2,1)S(1)}, u32[]{:S(2)}, u32[]{:S(2)}) collective-permute-start(bf16[336,128]{1,0:T(8,128)(2,1)S(1)} %get-tuple-element.245), channel_id=1, source_target_pairs={{0,30},{2,28},{4,26},{6,24},{8,22},{10,20},{12,18},{14,16},{16,14}... | collective-permute-start | bytes 258056 | tf_op jit(solution)/shard_map/cond/branch_5_fun/ppermute | solution.py:297
  33.5 1.8 %collective-permute-start.77 = (bf16[336,128]{1,0:T(8,128)(2,1)S(1)}, bf16[336,128]{1,0:T(8,128)(2,1)S(1)}, u32[]{:S(2)}, u32[]{:S(2)}) collective-permute-start(bf16[336,128]{1,0:T(8,128)(2,1)S(1)} %get-tuple-element.247), channel_id=1, source_target_pairs={{0,28},{2,30},{4,24},{6,26},{8,20},{10,22},{12,16},{14,18},{16,12}... | collective-permute-start | bytes 258056 | tf_op jit(solution)/shard_map/cond/branch_5_fun/ppermute | solution.py:297
  35.2 1.2 %collective-permute-start.78 = (bf16[336,128]{1,0:T(8,128)(2,1)S(1)}, bf16[336,128]{1,0:T(8,128)(2,1)S(1)}, u32[]{:S(2)}, u32[]{:S(2)}) collective-permute-start(bf16[336,128]{1,0:T(8,128)(2,1)S(1)} %get-tuple-element.248), channel_id=1, source_target_pairs={{0,12},{2,14},{4,8},{6,10},{8,4},{10,6},{12,0},{14,2},{16,28},{18,... | collective-permute-start | bytes 258056 | tf_op jit(solution)/shard_map/cond/branch_5_fun/ppermute | solution.py:297
  36.4 0.6 %collective-permute-done.89.refs_14_ = bf16[336,128]{1,0:T(8,128)(2,1)S(1)} collective-permute-done((bf16[336,128]{1,0:T(8,128)(2,1)S(1)}, bf16[336,128]{1,0:T(8,128)(2,1)S(1)}, u32[]{:S(2)}, u32[]{:S(2)}) %collective-permute-start.89) | collective-permute-done | bytes 86048 | tf_op jit(solution)/shard_map/cond/branch_5_fun/ppermute | solution.py:297
  37.0 3.1 %collective-permute-start.79 = (bf16[336,128]{1,0:T(8,128)(2,1)S(1)}, bf16[336,128]{1,0:T(8,128)(2,1)S(1)}, u32[]{:S(2)}, u32[]{:S(2)}) collective-permute-start(bf16[336,128]{1,0:T(8,128)(2,1)S(1)} %get-tuple-element.249), channel_id=1, source_target_pairs={{0,26},{2,24},{4,30},{6,28},{8,18},{10,16},{12,22},{14,20},{16,10}... | collective-permute-start | bytes 258056 | tf_op jit(solution)/shard_map/cond/branch_5_fun/ppermute | solution.py:297
  40.2 3.1 %collective-permute-start.80 = (bf16[336,128]{1,0:T(8,128)(2,1)S(1)}, bf16[336,128]{1,0:T(8,128)(2,1)S(1)}, u32[]{:S(2)}, u32[]{:S(2)}) collective-permute-start(bf16[336,128]{1,0:T(8,128)(2,1)S(1)} %get-tuple-element.250), channel_id=1, source_target_pairs={{0,10},{2,8},{4,14},{6,12},{8,2},{10,0},{12,6},{14,4},{16,26},{18,... | collective-permute-start | bytes 258056 | tf_op jit(solution)/shard_map/cond/branch_5_fun/ppermute | solution.py:297
  43.3 0.7 %collective-permute-start.81 = (bf16[336,128]{1,0:T(8,128)(2,1)S(1)}, bf16[336,128]{1,0:T(8,128)(2,1)S(1)}, u32[]{:S(2)}, u32[]{:S(2)}) collective-permute-start(bf16[336,128]{1,0:T(8,128)(2,1)S(1)} %get-tuple-element.251), channel_id=1, source_target_pairs={{0,24},{2,26},{4,28},{6,30},{8,16},{10,18},{12,20},{14,22},{16,8},... | collective-permute-start | bytes 258056 | tf_op jit(solution)/shard_map/cond/branch_5_fun/ppermute | solution.py:297
  44.0 1.1 %collective-permute-start.82 = (bf16[336,128]{1,0:T(8,128)(2,1)S(1)}, bf16[336,128]{1,0:T(8,128)(2,1)S(1)}, u32[]{:S(2)}, u32[]{:S(2)}) collective-permute-start(bf16[336,128]{1,0:T(8,128)(2,1)S(1)} %get-tuple-element.252), channel_id=1, source_target_pairs={{0,8},{2,10},{4,12},{6,14},{8,0},{10,2},{12,4},{14,6},{16,24},{18,... | collective-permute-start | bytes 258056 | tf_op jit(solution)/shard_map/cond/branch_5_fun/ppermute | solution.py:297
  45.1 2.1 %collective-permute-done.80.refs_5_ = bf16[336,128]{1,0:T(8,128)(2,1)S(1)} collective-permute-done((bf16[336,128]{1,0:T(8,128)(2,1)S(1)}, bf16[336,128]{1,0:T(8,128)(2,1)S(1)}, u32[]{:S(2)}, u32[]{:S(2)}) %collective-permute-start.80) | collective-permute-done | bytes 86048 | tf_op jit(solution)/shard_map/cond/branch_5_fun/ppermute | solution.py:297
  47.2 2.4 %collective-permute-done.81.refs_6_ = bf16[336,128]{1,0:T(8,128)(2,1)S(1)} collective-permute-done((bf16[336,128]{1,0:T(8,128)(2,1)S(1)}, bf16[336,128]{1,0:T(8,128)(2,1)S(1)}, u32[]{:S(2)}, u32[]{:S(2)}) %collective-permute-start.81) | collective-permute-done | bytes 86048 | tf_op jit(solution)/shard_map/cond/branch_5_fun/ppermute | solution.py:297
  49.6 3.5 %gram.20 = f32[128,128]{1,0:T(8,128)S(1)} custom-call(s32[6]{0:T(128)S(1)} %get-tuple-element.241.scalar_ref, bf16[336,128]{1,0:T(8,128)(2,1)S(1)} %collective-permute-done.75.refs_0_, bf16[336,128]{1,0:T(8,128)(2,1)S(1)} %collective-permute-done.76.refs_1_, bf16[336,128]{1,0:T(8,128)(2,1)S(1)} %collective-permute-done.77.refs_2_, ...), custom_call_target="tpu_custom_call" | custom-call | tf_op jit(solution)/shard_map/cond/branch_5_fun/gram/pallas_call | solution.py:298
  53.6 0.0 copy-start.4
  53.7 0.6 %copy-done.4 = f32[128,128]{1,0:T(8,128)} copy-done((f32[128,128]{1,0:T(8,128)}, f32[128,128]{1,0:T(8,128)S(1)}, u32[]{:S(2)}) %copy-start.4) | copy-done | bytes 65560
  (17 shorter events, 0.0 us)
Async XLA Ops:
  0.0 4.8 %collective-permute-start.225 = (bf16[8,1152,128]{2,1,0:T(8,128)(2,1)}, bf16[8,1152,128]{2,1,0:T(8,128)(2,1)S(1)}, u32[]{:S(2)}, u32[]{:S(2)}) collective-permute-start(bf16[8,1152,128]{2,1,0:T(8,128)(2,1)} %in_ref.1), channel_id=1, source_target_pairs={{0,1},{1,0},{2,3},{3,2},{4,5},{5,4},{6,7},{7,6},{8,9},{9,8},{10,11... | collective-permute-start | bytes 7077896 | tf_op jit(solution)/shard_map/ppermute | solution.py:254
  0.5 1.7 %copy-start = (bf16[8,1152,128]{2,1,0:T(8,128)(2,1)S(1)}, bf16[8,1152,128]{2,1,0:T(8,128)(2,1)}, u32[]{:S(2)}) copy-start(bf16[8,1152,128]{2,1,0:T(8,128)(2,1)} %in_ref.1) | copy-start | bytes 7077892
  2.1 0.7 %copy-start.1 = (s32[2304]{0:T(1024)S(1)}, s32[2304]{0:T(1024)}, u32[]{:S(2)}) copy-start(s32[2304]{0:T(1024)} %cycle_in.1) | copy-start | bytes 27652
  2.1 0.7 %copy-start.2 = (s32[2304]{0:T(1024)S(1)}, s32[2304]{0:T(1024)}, u32[]{:S(2)}) copy-start(s32[2304]{0:T(1024)} %valid_in.1) | copy-start | bytes 27652
  2.1 0.7 %copy-start.3 = (s32[32]{0:T(128)S(1)}, s32[32]{0:T(128)}, u32[]{:S(2)}) copy-start(s32[32]{0:T(128)} %owner_in.1) | copy-start | bytes 388
  10.4 16.6 %collective-permute-start.83 = (bf16[336,128]{1,0:T(8,128)(2,1)S(1)}, bf16[336,128]{1,0:T(8,128)(2,1)S(1)}, u32[]{:S(2)}, u32[]{:S(2)}) collective-permute-start(bf16[336,128]{1,0:T(8,128)(2,1)S(1)} %get-tuple-element.253), channel_id=1, source_target_pairs={{0,22},{2,20},{4,18},{6,16},{8,30},{10,28},{12,26},{14,24},{16,6},... | collective-permute-start | bytes 258056 | tf_op jit(solution)/shard_map/cond/branch_5_fun/ppermute | solution.py:297
  16.3 11.3 %collective-permute-start.84 = (bf16[336,128]{1,0:T(8,128)(2,1)S(1)}, bf16[336,128]{1,0:T(8,128)(2,1)S(1)}, u32[]{:S(2)}, u32[]{:S(2)}) collective-permute-start(bf16[336,128]{1,0:T(8,128)(2,1)S(1)} %get-tuple-element.254), channel_id=1, source_target_pairs={{0,6},{2,4},{4,2},{6,0},{8,14},{10,12},{12,10},{14,8},{16,22},{18,... | collective-permute-start | bytes 258056 | tf_op jit(solution)/shard_map/cond/branch_5_fun/ppermute | solution.py:297
  16.8 11.0 %collective-permute-start.85 = (bf16[336,128]{1,0:T(8,128)(2,1)S(1)}, bf16[336,128]{1,0:T(8,128)(2,1)S(1)}, u32[]{:S(2)}, u32[]{:S(2)}) collective-permute-start(bf16[336,128]{1,0:T(8,128)(2,1)S(1)} %get-tuple-element.255), channel_id=1, source_target_pairs={{0,20},{2,22},{4,16},{6,18},{8,28},{10,30},{12,24},{14,26},{16,4},... | collective-permute-start | bytes 258056 | tf_op jit(solution)/shard_map/cond/branch_5_fun/ppermute | solution.py:297
  18.1 15.4 %collective-permute-start.86 = (bf16[336,128]{1,0:T(8,128)(2,1)S(1)}, bf16[336,128]{1,0:T(8,128)(2,1)S(1)}, u32[]{:S(2)}, u32[]{:S(2)}) collective-permute-start(bf16[336,128]{1,0:T(8,128)(2,1)S(1)} %get-tuple-element.256), channel_id=1, source_target_pairs={{0,4},{2,6},{4,0},{6,2},{8,12},{10,14},{12,8},{14,10},{16,20},{18,... | collective-permute-start | bytes 258056 | tf_op jit(solution)/shard_map/cond/branch_5_fun/ppermute | solution.py:297
  18.4 15.0 %collective-permute-start.87 = (bf16[336,128]{1,0:T(8,128)(2,1)S(1)}, bf16[336,128]{1,0:T(8,128)(2,1)S(1)}, u32[]{:S(2)}, u32[]{:S(2)}) collective-permute-start(bf16[336,128]{1,0:T(8,128)(2,1)S(1)} %get-tuple-element.257), channel_id=1, source_target_pairs={{0,18},{2,16},{4,22},{6,20},{8,26},{10,24},{12,30},{14,28},{16,2},... | collective-permute-start | bytes 258056 | tf_op jit(solution)/shard_map/cond/branch_5_fun/ppermute | solution.py:297
  27.0 8.2 %collective-permute-start.88 = (bf16[336,128]{1,0:T(8,128)(2,1)S(1)}, bf16[336,128]{1,0:T(8,128)(2,1)S(1)}, u32[]{:S(2)}, u32[]{:S(2)}) collective-permute-start(bf16[336,128]{1,0:T(8,128)(2,1)S(1)} %get-tuple-element.258), channel_id=1, source_target_pairs={{0,2},{2,0},{4,6},{6,4},{8,10},{10,8},{12,14},{14,12},{16,18},{18,... | collective-permute-start | bytes 258056 | tf_op jit(solution)/shard_map/cond/branch_5_fun/ppermute | solution.py:297
  27.6 9.4 %collective-permute-start.89 = (bf16[336,128]{1,0:T(8,128)(2,1)S(1)}, bf16[336,128]{1,0:T(8,128)(2,1)S(1)}, u32[]{:S(2)}, u32[]{:S(2)}) collective-permute-start(bf16[336,128]{1,0:T(8,128)(2,1)S(1)} %get-tuple-element.259), channel_id=1, source_target_pairs={{0,16},{2,18},{4,20},{6,22},{8,24},{10,26},{12,28},{14,30},{16,0},... | collective-permute-start | bytes 258056 | tf_op jit(solution)/shard_map/cond/branch_5_fun/ppermute | solution.py:297
  27.8 12.4 %collective-permute-start.75 = (bf16[336,128]{1,0:T(8,128)(2,1)S(1)}, bf16[336,128]{1,0:T(8,128)(2,1)S(1)}, u32[]{:S(2)}, u32[]{:S(2)}) collective-permute-start(bf16[336,128]{1,0:T(8,128)(2,1)S(1)} %get-tuple-element.245), channel_id=1, source_target_pairs={{0,30},{2,28},{4,26},{6,24},{8,22},{10,20},{12,18},{14,16},{16,14}... | collective-permute-start | bytes 258056 | tf_op jit(solution)/shard_map/cond/branch_5_fun/ppermute | solution.py:297
  33.4 9.8 %collective-permute-start.76 = (bf16[336,128]{1,0:T(8,128)(2,1)S(1)}, bf16[336,128]{1,0:T(8,128)(2,1)S(1)}, u32[]{:S(2)}, u32[]{:S(2)}) collective-permute-start(bf16[336,128]{1,0:T(8,128)(2,1)S(1)} %get-tuple-element.246), channel_id=1, source_target_pairs={{0,14},{2,12},{4,10},{6,8},{8,6},{10,4},{12,2},{14,0},{16,30},{18,... | collective-permute-start | bytes 258056 | tf_op jit(solution)/shard_map/cond/branch_5_fun/ppermute | solution.py:297
  33.5 10.6 %collective-permute-start.77 = (bf16[336,128]{1,0:T(8,128)(2,1)S(1)}, bf16[336,128]{1,0:T(8,128)(2,1)S(1)}, u32[]{:S(2)}, u32[]{:S(2)}) collective-permute-start(bf16[336,128]{1,0:T(8,128)(2,1)S(1)} %get-tuple-element.247), channel_id=1, source_target_pairs={{0,28},{2,30},{4,24},{6,26},{8,20},{10,22},{12,16},{14,18},{16,12}... | collective-permute-start | bytes 258056 | tf_op jit(solution)/shard_map/cond/branch_5_fun/ppermute | solution.py:297
  35.2 9.9 %collective-permute-start.78 = (bf16[336,128]{1,0:T(8,128)(2,1)S(1)}, bf16[336,128]{1,0:T(8,128)(2,1)S(1)}, u32[]{:S(2)}, u32[]{:S(2)}) collective-permute-start(bf16[336,128]{1,0:T(8,128)(2,1)S(1)} %get-tuple-element.248), channel_id=1, source_target_pairs={{0,12},{2,14},{4,8},{6,10},{8,4},{10,6},{12,0},{14,2},{16,28},{18,... | collective-permute-start | bytes 258056 | tf_op jit(solution)/shard_map/cond/branch_5_fun/ppermute | solution.py:297
  37.0 8.1 %collective-permute-start.79 = (bf16[336,128]{1,0:T(8,128)(2,1)S(1)}, bf16[336,128]{1,0:T(8,128)(2,1)S(1)}, u32[]{:S(2)}, u32[]{:S(2)}) collective-permute-start(bf16[336,128]{1,0:T(8,128)(2,1)S(1)} %get-tuple-element.249), channel_id=1, source_target_pairs={{0,26},{2,24},{4,30},{6,28},{8,18},{10,16},{12,22},{14,20},{16,10}... | collective-permute-start | bytes 258056 | tf_op jit(solution)/shard_map/cond/branch_5_fun/ppermute | solution.py:297
  40.2 7.0 %collective-permute-start.80 = (bf16[336,128]{1,0:T(8,128)(2,1)S(1)}, bf16[336,128]{1,0:T(8,128)(2,1)S(1)}, u32[]{:S(2)}, u32[]{:S(2)}) collective-permute-start(bf16[336,128]{1,0:T(8,128)(2,1)S(1)} %get-tuple-element.250), channel_id=1, source_target_pairs={{0,10},{2,8},{4,14},{6,12},{8,2},{10,0},{12,6},{14,4},{16,26},{18,... | collective-permute-start | bytes 258056 | tf_op jit(solution)/shard_map/cond/branch_5_fun/ppermute | solution.py:297
  43.3 6.3 %collective-permute-start.81 = (bf16[336,128]{1,0:T(8,128)(2,1)S(1)}, bf16[336,128]{1,0:T(8,128)(2,1)S(1)}, u32[]{:S(2)}, u32[]{:S(2)}) collective-permute-start(bf16[336,128]{1,0:T(8,128)(2,1)S(1)} %get-tuple-element.251), channel_id=1, source_target_pairs={{0,24},{2,26},{4,28},{6,30},{8,16},{10,18},{12,20},{14,22},{16,8},... | collective-permute-start | bytes 258056 | tf_op jit(solution)/shard_map/cond/branch_5_fun/ppermute | solution.py:297
  44.0 5.6 %collective-permute-start.82 = (bf16[336,128]{1,0:T(8,128)(2,1)S(1)}, bf16[336,128]{1,0:T(8,128)(2,1)S(1)}, u32[]{:S(2)}, u32[]{:S(2)}) collective-permute-start(bf16[336,128]{1,0:T(8,128)(2,1)S(1)} %get-tuple-element.252), channel_id=1, source_target_pairs={{0,8},{2,10},{4,12},{6,14},{8,0},{10,2},{12,4},{14,6},{16,24},{18,... | collective-permute-start | bytes 258056 | tf_op jit(solution)/shard_map/cond/branch_5_fun/ppermute | solution.py:297
  53.6 0.6 %copy-start.4 = (f32[128,128]{1,0:T(8,128)}, f32[128,128]{1,0:T(8,128)S(1)}, u32[]{:S(2)}) copy-start(f32[128,128]{1,0:T(8,128)S(1)} %get-tuple-element.928) | copy-start | bytes 196612

commit v6 on v5

--- a/solution.py
+++ b/solution.py
@@ -9,8 +9,8 @@
 
 LANE = 128
 UNROLL = 16
-GROUPS = 2
-STEP = 384
+GROUPS = 4
+STEP = 128
 VMEM_LIMIT = 24 * 1024 * 1024
 LADDER = (16, 24, 32, 36, 40, 42, 44, 46, 48, 52, 56, 64, 80, 104, 144)
 NT = (((1,), (1,)), ((), ()))
@@ -129,22 +129,20 @@
 
 def widen_kernel(in_ref, out_ref):
     frames, half, _ = in_ref.shape
-    for f in range(frames):
-
-        def widen(i, _, f=f):
-            begin = pl.multiple_of(i * STEP, STEP)
-            rows = in_ref[f, pl.ds(begin, STEP), :].astype(jnp.float32)
-            out_ref[pl.ds(f * (half + 1) + begin, STEP), :] = rows
-            return 0
-
-        lax.fori_loop(0, half // STEP, widen, 0)
-
-
-def pack_kernel(group, word_ref, scalar_ref, near_ref, far_ref, *rest):
+
+    def widen(i, _):
+        begin = pl.multiple_of(i * STEP, STEP)
+        rows = in_ref[:, pl.ds(begin, STEP), :].astype(jnp.float32)
+        out_ref[pl.ds(begin, STEP)] = jnp.transpose(rows, (1, 0, 2))
+        return 0
+
+    lax.fori_loop(0, half // STEP, widen, 0)
+
+
+def pack_kernel(group, word_ref, scalar_ref, near_ref, far_ref, after_ref, *rest):
     out_refs, stage = rest[:-1], rest[-1]
     depth = out_refs[0].shape[0]
-    frames = 8
-    stride = near_ref.shape[0] // frames
+    frames = near_ref.shape[1]
     first_row = group * len(out_refs) * (depth // frames)
     lane = lax.broadcasted_iota(jnp.int32, (frames, LANE), 1)
 
@@ -153,8 +151,8 @@
         turned, row, shift = [], [], []
         for j in range(count):
             word = word_ref[i + j]
-            at = pl.ds(word & 2047, frames, stride=stride)
-            x = jnp.where((word & 2048) == 0, near_ref[at, :], far_ref[at, :])
+            block = word & 2047
+            x = jnp.where((word & 2048) == 0, near_ref[block], far_ref[block])
             row.append((word >> 19) - first_row)
             shift.append((word >> 12) & (LANE - 1))
             turned.append(pltpu.roll(x, shift[j], 1))
@@ -244,7 +242,7 @@
     def widen(part):
         return pl.pallas_call(
             widen_kernel,
-            out_shape=jax.ShapeDtypeStruct((local_frames * (half + 1), LANE), jnp.float32),
+            out_shape=jax.ShapeDtypeStruct((half, local_frames, LANE), jnp.float32),
             in_specs=[vmem],
             out_specs=vmem,
             compiler_params=params,
@@ -278,11 +276,12 @@
 
         def run(words, scalars, near_pool, far_pool):
             got = []
+            after = scalars
             for group in range(GROUPS):
                 send = pl.pallas_call(
                     functools.partial(pack_kernel, group),
                     out_shape=(jax.ShapeDtypeStruct((depth, LANE), jnp.bfloat16),) * members,
-                    in_specs=[smem, smem, vmem, vmem],
+                    in_specs=[smem, smem, vmem, vmem, pl.BlockSpec(memory_space=pl.ANY)],
                     out_specs=(vmem,) * members,
                     scratch_shapes=[pltpu.VMEM((members * depth + local_frames, LANE), jnp.float32)],
                     compiler_params=params,
@@ -290,7 +289,8 @@
                         flops=2_000_000, bytes_accessed=16_000_000, transcendentals=0
                     ),
                     name="pack",
-                )(words, scalars, near_pool, far_pool)
+                )(words, scalars, near_pool, far_pool, after)
+                after = send[-1]
                 for j in range(members):
                     apart = apart_of(group * members + j, tm_count)
                     pairs = [(i, i ^ apart) for i in range(tm_count)]

time: 54.5 us -> 56.6 us (1.039)
  Pallas kernels: 16 us -> 18.9 us
  starting transfers between devices: 29.6 us -> 27.3 us
  waiting for transfers between devices: 5.19 us -> 6.94 us
    ppermute x15, starting transfers between devices: 29.2 us -> 26.8 us  [run(): got.append(lax.ppermute(send[j], 'tm', pairs) if apart else send[j])]
    ppermute x15, waiting for transfers between devices: 5.07 us -> 6.94 us  [run(): got.append(lax.ppermute(send[j], 'tm', pairs) if apart else send[j])]
    pallas_call x2 -> x4, Pallas kernels: 9.83 us -> 11.6 us  [run(): pl.pallas_call(functools.partial(pack_kernel, group), out_shape=(jax.Shap...]
    pallas_call x2, Pallas kernels: 0.8 us -> 1.94 us  [widen(): pl.pallas_call(widen_kernel, out_shape=jax.ShapeDtypeStruct((half, local_...]
  transfers between devices with their start and end apart: 16 -> 16, of which waited for: 4 -> 3; matrix products, arithmetic and copies ran while one was open for 0% -> 0% of each run, Pallas kernels for 13% -> 20%
where the time goes in v6:
time: 56.6 us; the launch traced here: 56.3 us
  starting transfers between devices  27.3 us (48%)
  Pallas kernels  18.9 us (33%)
  waiting for transfers between devices  6.94 us (12%)
  local copies, waits for them, and re-layouts  2.3 us (4%)
  loops' own time  0.81 us (1%)
    ppermute x15, starting transfers between devices, run(): got.append(lax.ppermute(send[j], 'tm', pairs) if apart else send[j])  26.8 us
    pallas_call x4, Pallas kernels, run(): pl.pallas_call(functools.partial(pack_kernel, group), out_shape=(jax.Shap...  11.6 us
    ppermute x15, waiting for transfers between devices, run(): got.append(lax.ppermute(send[j], 'tm', pairs) if apart else send[j])  6.94 us
    pallas_call x1, Pallas kernels, run(): pl.pallas_call(gram_kernel, out_shape=jax.ShapeDtypeStruct((frame_count,...  3.55 us
    unnamed x10, local copies, waits for them, and re-layouts  2.3 us
    pallas_call x2, Pallas kernels, widen(): pl.pallas_call(widen_kernel, out_shape=jax.ShapeDtypeStruct((half, local_...  1.94 us
    pallas_call x1, Pallas kernels, on_device_routed(): pl.pallas_call(plan_kernel, out_shape=(jax.ShapeDtypeStruct((list_rows, L...  1.82 us
  transfers between devices with their start and end apart: 16, of which 3 were waited for; matrix products, arithmetic and copies ran while one was open for 0% of the time, Pallas kernels for 20%

profile of v6, /device:TPU:0, one launch (start us, length us, event | category | flops | bytes accessed | tf_op | source)
XLA Modules:
  0.0 56.3 jit_solution(7516128474563850528)
XLA Ops:
  0.0 0.5 collective-permute-start.225
  0.5 1.7 %copy-done = bf16[8,1152,128]{2,1,0:T(8,128)(2,1)S(1)} copy-done((bf16[8,1152,128]{2,1,0:T(8,128)(2,1)S(1)}, bf16[8,1152,128]{2,1,0:T(8,128)(2,1)}, u32[]{:S(2)}) %copy-start) | copy-done | bytes 2359320
  2.1 1.0 %widen.2 = f32[1152,8,128]{2,1,0:T(8,128)S(1)} custom-call(bf16[8,1152,128]{2,1,0:T(8,128)(2,1)S(1)} %copy-done), custom_call_target="tpu_custom_call" | custom-call | tf_op jit(solution)/shard_map/widen/pallas_call | solution.py:243
  3.1 1.8 %plan.1 = (s32[24,128]{1,0:T(8,128)S(1)}, s32[8]{0:T(128)S(1)}) custom-call(s32[32]{0:T(128)S(1)} %copy-done.3, s32[2304]{0:T(1024)S(1)} %copy-done.1, s32[2304]{0:T(1024)S(1)} %copy-done.2), custom_call_target="tpu_custom_call" | custom-call | tf_op jit(solution)/shard_map/plan/pallas_call | solution.py:253
  5.0 0.0 collective-permute-done.225.in_ref
  5.0 1.0 %widen.3 = f32[1152,8,128]{2,1,0:T(8,128)S(1)} custom-call(bf16[8,1152,128]{2,1,0:T(8,128)(2,1)S(1)} %collective-permute-done.225.in_ref), custom_call_target="tpu_custom_call" | custom-call | tf_op jit(solution)/shard_map/widen/pallas_call | solution.py:243
  6.0 49.7 %conditional.1 = (f32[128,128]{1,0:T(8,128)S(1)}) conditional(s32[]{:T(128)} %bitcast.15, (s32[24,128]{1,0:T(8,128)S(1)}, s32[8]{0:T(128)S(1)}, f32[1152,8,128]{2,1,0:T(8,128)S(1)}, f32[1152,8,128]{2,1,0:T(8,128)S(1)}) %tuple.50, (s32[24,128]{1,0:T(8,128)S(1)}, s32[8]{0:T(128)S(1)}, f32[1152,8,128]{2,1,0:T(8,128)S(1)}, ...), branch_computations={%region_0.0_spmd, %region_1.0_spmd, %region_2.0_spmd, %region_3.0_... | conditional | flops 8000000 | bytes 81695328 | solution.py:310
  6.2 2.9 %pack.80 = (bf16[336,128]{1,0:T(8,128)(2,1)S(1)}, bf16[336,128]{1,0:T(8,128)(2,1)S(1)}, bf16[336,128]{1,0:T(8,128)(2,1)S(1)}, bf16[336,128]{1,0:T(8,128)(2,1)S(1)}) custom-call(s32[3072]{0:T(1024)S(1)} %bitcast.37, s32[8]{0:T(128)S(1)} %get-tuple-element.241.scalar_ref.after_ref, f32[1152,8,128]{2,1,0:T(8,128)S(1)} %get-tuple-element.243.near_ref, ...), custom_call_target="tpu_custom_call" | custom-call | flops 2000000 | bytes 16000000 | tf_op jit(solution)/shard_map/cond/branch_5_fun/pack/pallas_call | solution.py:281
  9.1 6.7 %collective-permute-start.75 = (bf16[336,128]{1,0:T(8,128)(2,1)S(1)}, bf16[336,128]{1,0:T(8,128)(2,1)S(1)}, u32[]{:S(2)}, u32[]{:S(2)}) collective-permute-start(bf16[336,128]{1,0:T(8,128)(2,1)S(1)} %get-tuple-element.245), channel_id=1, source_target_pairs={{0,30},{2,28},{4,26},{6,24},{8,22},{10,20},{12,18},{14,16},{16,14}... | collective-permute-start | bytes 258056 | tf_op jit(solution)/shard_map/cond/branch_5_fun/ppermute | solution.py:297
  15.8 0.0 collective-permute-start.76
  15.8 1.8 %collective-permute-start.77 = (bf16[336,128]{1,0:T(8,128)(2,1)S(1)}, bf16[336,128]{1,0:T(8,128)(2,1)S(1)}, u32[]{:S(2)}, u32[]{:S(2)}) collective-permute-start(bf16[336,128]{1,0:T(8,128)(2,1)S(1)} %get-tuple-element.247), channel_id=1, source_target_pairs={{0,28},{2,30},{4,24},{6,26},{8,20},{10,22},{12,16},{14,18},{16,12}... | collective-permute-start | bytes 258056 | tf_op jit(solution)/shard_map/cond/branch_5_fun/ppermute | solution.py:297
  17.6 1.1 %collective-permute-start.78 = (bf16[336,128]{1,0:T(8,128)(2,1)S(1)}, bf16[336,128]{1,0:T(8,128)(2,1)S(1)}, u32[]{:S(2)}, u32[]{:S(2)}) collective-permute-start(bf16[336,128]{1,0:T(8,128)(2,1)S(1)} %get-tuple-element.248.after_ref), channel_id=1, source_target_pairs={{0,12},{2,14},{4,8},{6,10},{8,4},{10,6},{12,0},{14,2},{16,28},{18,... | collective-permute-start | bytes 258056 | tf_op jit(solution)/shard_map/cond/branch_5_fun/ppermute | solution.py:297
  18.7 2.9 %pack.81 = (bf16[336,128]{1,0:T(8,128)(2,1)S(1)}, bf16[336,128]{1,0:T(8,128)(2,1)S(1)}, bf16[336,128]{1,0:T(8,128)(2,1)S(1)}, bf16[336,128]{1,0:T(8,128)(2,1)S(1)}) custom-call(s32[3072]{0:T(1024)S(1)} %bitcast.38, s32[8]{0:T(128)S(1)} %get-tuple-element.241.scalar_ref.after_ref, f32[1152,8,128]{2,1,0:T(8,128)S(1)} %get-tuple-element.243.near_ref, ...), custom_call_target="tpu_custom_call" | custom-call | flops 2000000 | bytes 16000000 | tf_op jit(solution)/shard_map/cond/branch_5_fun/pack/pallas_call | solution.py:281
  21.6 3.9 %collective-permute-start.79 = (bf16[336,128]{1,0:T(8,128)(2,1)S(1)}, bf16[336,128]{1,0:T(8,128)(2,1)S(1)}, u32[]{:S(2)}, u32[]{:S(2)}) collective-permute-start(bf16[336,128]{1,0:T(8,128)(2,1)S(1)} %get-tuple-element.249), channel_id=1, source_target_pairs={{0,26},{2,24},{4,30},{6,28},{8,18},{10,16},{12,22},{14,20},{16,10}... | collective-permute-start | bytes 258056 | tf_op jit(solution)/shard_map/cond/branch_5_fun/ppermute | solution.py:297
  25.5 0.1 collective-permute-start.80
  25.6 1.0 %collective-permute-start.81 = (bf16[336,128]{1,0:T(8,128)(2,1)S(1)}, bf16[336,128]{1,0:T(8,128)(2,1)S(1)}, u32[]{:S(2)}, u32[]{:S(2)}) collective-permute-start(bf16[336,128]{1,0:T(8,128)(2,1)S(1)} %get-tuple-element.251), channel_id=1, source_target_pairs={{0,24},{2,26},{4,28},{6,30},{8,16},{10,18},{12,20},{14,22},{16,8},... | collective-permute-start | bytes 258056 | tf_op jit(solution)/shard_map/cond/branch_5_fun/ppermute | solution.py:297
  26.5 2.9 %pack.82 = (bf16[336,128]{1,0:T(8,128)(2,1)S(1)}, bf16[336,128]{1,0:T(8,128)(2,1)S(1)}, bf16[336,128]{1,0:T(8,128)(2,1)S(1)}, bf16[336,128]{1,0:T(8,128)(2,1)S(1)}) custom-call(s32[3072]{0:T(1024)S(1)} %bitcast.39, s32[8]{0:T(128)S(1)} %get-tuple-element.241.scalar_ref.after_ref, f32[1152,8,128]{2,1,0:T(8,128)S(1)} %get-tuple-element.243.near_ref, ...), custom_call_target="tpu_custom_call" | custom-call | flops 2000000 | bytes 16000000 | tf_op jit(solution)/shard_map/cond/branch_5_fun/pack/pallas_call | solution.py:281
  29.4 1.1 %collective-permute-start.82 = (bf16[336,128]{1,0:T(8,128)(2,1)S(1)}, bf16[336,128]{1,0:T(8,128)(2,1)S(1)}, u32[]{:S(2)}, u32[]{:S(2)}) collective-permute-start(bf16[336,128]{1,0:T(8,128)(2,1)S(1)} %get-tuple-element.252.after_ref), channel_id=1, source_target_pairs={{0,8},{2,10},{4,12},{6,14},{8,0},{10,2},{12,4},{14,6},{16,24},{18,... | collective-permute-start | bytes 258056 | tf_op jit(solution)/shard_map/cond/branch_5_fun/ppermute | solution.py:297
  30.5 3.7 %collective-permute-start.83 = (bf16[336,128]{1,0:T(8,128)(2,1)S(1)}, bf16[336,128]{1,0:T(8,128)(2,1)S(1)}, u32[]{:S(2)}, u32[]{:S(2)}) collective-permute-start(bf16[336,128]{1,0:T(8,128)(2,1)S(1)} %get-tuple-element.253), channel_id=1, source_target_pairs={{0,22},{2,20},{4,18},{6,16},{8,30},{10,28},{12,26},{14,24},{16,6},... | collective-permute-start | bytes 258056 | tf_op jit(solution)/shard_map/cond/branch_5_fun/ppermute | solution.py:297
  34.3 1.0 %collective-permute-start.84 = (bf16[336,128]{1,0:T(8,128)(2,1)S(1)}, bf16[336,128]{1,0:T(8,128)(2,1)S(1)}, u32[]{:S(2)}, u32[]{:S(2)}) collective-permute-start(bf16[336,128]{1,0:T(8,128)(2,1)S(1)} %get-tuple-element.254), channel_id=1, source_target_pairs={{0,6},{2,4},{4,2},{6,0},{8,14},{10,12},{12,10},{14,8},{16,22},{18,... | collective-permute-start | bytes 258056 | tf_op jit(solution)/shard_map/cond/branch_5_fun/ppermute | solution.py:297
  35.3 2.9 %pack.83 = (bf16[336,128]{1,0:T(8,128)(2,1)S(1)}, bf16[336,128]{1,0:T(8,128)(2,1)S(1)}, bf16[336,128]{1,0:T(8,128)(2,1)S(1)}, bf16[336,128]{1,0:T(8,128)(2,1)S(1)}) custom-call(s32[3072]{0:T(1024)S(1)} %bitcast.40, s32[8]{0:T(128)S(1)} %get-tuple-element.241.scalar_ref.after_ref, f32[1152,8,128]{2,1,0:T(8,128)S(1)} %get-tuple-element.243.near_ref, ...), custom_call_target="tpu_custom_call" | custom-call | flops 2000000 | bytes 16000000 | tf_op jit(solution)/shard_map/cond/branch_5_fun/pack/pallas_call | solution.py:281
  38.2 1.5 %collective-permute-start.85 = (bf16[336,128]{1,0:T(8,128)(2,1)S(1)}, bf16[336,128]{1,0:T(8,128)(2,1)S(1)}, u32[]{:S(2)}, u32[]{:S(2)}) collective-permute-start(bf16[336,128]{1,0:T(8,128)(2,1)S(1)} %get-tuple-element.255), channel_id=1, source_target_pairs={{0,20},{2,22},{4,16},{6,18},{8,28},{10,30},{12,24},{14,26},{16,4},... | collective-permute-start | bytes 258056 | tf_op jit(solution)/shard_map/cond/branch_5_fun/ppermute | solution.py:297
  39.7 2.8 %collective-permute-start.87 = (bf16[336,128]{1,0:T(8,128)(2,1)S(1)}, bf16[336,128]{1,0:T(8,128)(2,1)S(1)}, u32[]{:S(2)}, u32[]{:S(2)}) collective-permute-start(bf16[336,128]{1,0:T(8,128)(2,1)S(1)} %get-tuple-element.257), channel_id=1, source_target_pairs={{0,18},{2,16},{4,22},{6,20},{8,26},{10,24},{12,30},{14,28},{16,2},... | collective-permute-start | bytes 258056 | tf_op jit(solution)/shard_map/cond/branch_5_fun/ppermute | solution.py:297
  42.5 1.1 %collective-permute-start.88 = (bf16[336,128]{1,0:T(8,128)(2,1)S(1)}, bf16[336,128]{1,0:T(8,128)(2,1)S(1)}, u32[]{:S(2)}, u32[]{:S(2)}) collective-permute-start(bf16[336,128]{1,0:T(8,128)(2,1)S(1)} %get-tuple-element.258), channel_id=1, source_target_pairs={{0,2},{2,0},{4,6},{6,4},{8,10},{10,8},{12,14},{14,12},{16,18},{18,... | collective-permute-start | bytes 258056 | tf_op jit(solution)/shard_map/cond/branch_5_fun/ppermute | solution.py:297
  43.6 0.5 collective-permute-start.89
  44.1 0.6 %collective-permute-start.86 = (bf16[336,128]{1,0:T(8,128)(2,1)S(1)}, bf16[336,128]{1,0:T(8,128)(2,1)S(1)}, u32[]{:S(2)}, u32[]{:S(2)}) collective-permute-start(bf16[336,128]{1,0:T(8,128)(2,1)S(1)} %get-tuple-element.256.after_ref), channel_id=1, source_target_pairs={{0,4},{2,6},{4,0},{6,2},{8,12},{10,14},{12,8},{14,10},{16,20},{18,... | collective-permute-start | bytes 258056 | tf_op jit(solution)/shard_map/cond/branch_5_fun/ppermute | solution.py:297
  44.7 3.6 %collective-permute-done.85.refs_10_ = bf16[336,128]{1,0:T(8,128)(2,1)S(1)} collective-permute-done((bf16[336,128]{1,0:T(8,128)(2,1)S(1)}, bf16[336,128]{1,0:T(8,128)(2,1)S(1)}, u32[]{:S(2)}, u32[]{:S(2)}) %collective-permute-start.85) | collective-permute-done | bytes 86048 | tf_op jit(solution)/shard_map/cond/branch_5_fun/ppermute | solution.py:297
  48.3 2.5 %collective-permute-done.87.refs_12_ = bf16[336,128]{1,0:T(8,128)(2,1)S(1)} collective-permute-done((bf16[336,128]{1,0:T(8,128)(2,1)S(1)}, bf16[336,128]{1,0:T(8,128)(2,1)S(1)}, u32[]{:S(2)}, u32[]{:S(2)}) %collective-permute-start.87) | collective-permute-done | bytes 86048 | tf_op jit(solution)/shard_map/cond/branch_5_fun/ppermute | solution.py:297
  50.8 0.7 %collective-permute-done.89.refs_14_ = bf16[336,128]{1,0:T(8,128)(2,1)S(1)} collective-permute-done((bf16[336,128]{1,0:T(8,128)(2,1)S(1)}, bf16[336,128]{1,0:T(8,128)(2,1)S(1)}, u32[]{:S(2)}, u32[]{:S(2)}) %collective-permute-start.89) | collective-permute-done | bytes 86048 | tf_op jit(solution)/shard_map/cond/branch_5_fun/ppermute | solution.py:297
  51.6 3.5 %gram.20 = f32[128,128]{1,0:T(8,128)S(1)} custom-call(s32[8]{0:T(128)S(1)} %get-tuple-element.241.scalar_ref.after_ref, bf16[336,128]{1,0:T(8,128)(2,1)S(1)} %collective-permute-done.75.refs_0_, bf16[336,128]{1,0:T(8,128)(2,1)S(1)} %collective-permute-done.76.refs_1_, bf16[336,128]{1,0:T(8,128)(2,1)S(1)} %collective-permute-done.77.refs_2_, ...), custom_call_target="tpu_custom_call" | custom-call | tf_op jit(solution)/shard_map/cond/branch_5_fun/gram/pallas_call | solution.py:298
  55.7 0.0 copy-start.4
  55.7 0.6 %copy-done.4 = f32[128,128]{1,0:T(8,128)} copy-done((f32[128,128]{1,0:T(8,128)}, f32[128,128]{1,0:T(8,128)S(1)}, u32[]{:S(2)}) %copy-start.4) | copy-done | bytes 65560
  (19 shorter events, 0.0 us)
Async XLA Ops:
  0.0 5.0 %collective-permute-start.225 = (bf16[8,1152,128]{2,1,0:T(8,128)(2,1)}, bf16[8,1152,128]{2,1,0:T(8,128)(2,1)S(1)}, u32[]{:S(2)}, u32[]{:S(2)}) collective-permute-start(bf16[8,1152,128]{2,1,0:T(8,128)(2,1)} %in_ref.1), channel_id=1, source_target_pairs={{0,1},{1,0},{2,3},{3,2},{4,5},{5,4},{6,7},{7,6},{8,9},{9,8},{10,11... | collective-permute-start | bytes 7077896 | tf_op jit(solution)/shard_map/ppermute | solution.py:252
  0.5 1.7 %copy-start = (bf16[8,1152,128]{2,1,0:T(8,128)(2,1)S(1)}, bf16[8,1152,128]{2,1,0:T(8,128)(2,1)}, u32[]{:S(2)}) copy-start(bf16[8,1152,128]{2,1,0:T(8,128)(2,1)} %in_ref.1) | copy-start | bytes 7077892
  2.1 1.0 %copy-start.1 = (s32[2304]{0:T(1024)S(1)}, s32[2304]{0:T(1024)}, u32[]{:S(2)}) copy-start(s32[2304]{0:T(1024)} %cycle_in.1) | copy-start | bytes 27652
  2.1 1.0 %copy-start.2 = (s32[2304]{0:T(1024)S(1)}, s32[2304]{0:T(1024)}, u32[]{:S(2)}) copy-start(s32[2304]{0:T(1024)} %valid_in.1) | copy-start | bytes 27652
  2.1 1.0 %copy-start.3 = (s32[32]{0:T(128)S(1)}, s32[32]{0:T(128)}, u32[]{:S(2)}) copy-start(s32[32]{0:T(128)} %owner_in.1) | copy-start | bytes 388
  9.1 16.4 %collective-permute-start.75 = (bf16[336,128]{1,0:T(8,128)(2,1)S(1)}, bf16[336,128]{1,0:T(8,128)(2,1)S(1)}, u32[]{:S(2)}, u32[]{:S(2)}) collective-permute-start(bf16[336,128]{1,0:T(8,128)(2,1)S(1)} %get-tuple-element.245), channel_id=1, source_target_pairs={{0,30},{2,28},{4,26},{6,24},{8,22},{10,20},{12,18},{14,16},{16,14}... | collective-permute-start | bytes 258056 | tf_op jit(solution)/shard_map/cond/branch_5_fun/ppermute | solution.py:297
  15.8 9.7 %collective-permute-start.76 = (bf16[336,128]{1,0:T(8,128)(2,1)S(1)}, bf16[336,128]{1,0:T(8,128)(2,1)S(1)}, u32[]{:S(2)}, u32[]{:S(2)}) collective-permute-start(bf16[336,128]{1,0:T(8,128)(2,1)S(1)} %get-tuple-element.246), channel_id=1, source_target_pairs={{0,14},{2,12},{4,10},{6,8},{8,6},{10,4},{12,2},{14,0},{16,30},{18,... | collective-permute-start | bytes 258056 | tf_op jit(solution)/shard_map/cond/branch_5_fun/ppermute | solution.py:297
  15.8 13.6 %collective-permute-start.77 = (bf16[336,128]{1,0:T(8,128)(2,1)S(1)}, bf16[336,128]{1,0:T(8,128)(2,1)S(1)}, u32[]{:S(2)}, u32[]{:S(2)}) collective-permute-start(bf16[336,128]{1,0:T(8,128)(2,1)S(1)} %get-tuple-element.247), channel_id=1, source_target_pairs={{0,28},{2,30},{4,24},{6,26},{8,20},{10,22},{12,16},{14,18},{16,12}... | collective-permute-start | bytes 258056 | tf_op jit(solution)/shard_map/cond/branch_5_fun/ppermute | solution.py:297
  17.6 12.9 %collective-permute-start.78 = (bf16[336,128]{1,0:T(8,128)(2,1)S(1)}, bf16[336,128]{1,0:T(8,128)(2,1)S(1)}, u32[]{:S(2)}, u32[]{:S(2)}) collective-permute-start(bf16[336,128]{1,0:T(8,128)(2,1)S(1)} %get-tuple-element.248.after_ref), channel_id=1, source_target_pairs={{0,12},{2,14},{4,8},{6,10},{8,4},{10,6},{12,0},{14,2},{16,28},{18,... | collective-permute-start | bytes 258056 | tf_op jit(solution)/shard_map/cond/branch_5_fun/ppermute | solution.py:297
  21.6 12.6 %collective-permute-start.79 = (bf16[336,128]{1,0:T(8,128)(2,1)S(1)}, bf16[336,128]{1,0:T(8,128)(2,1)S(1)}, u32[]{:S(2)}, u32[]{:S(2)}) collective-permute-start(bf16[336,128]{1,0:T(8,128)(2,1)S(1)} %get-tuple-element.249), channel_id=1, source_target_pairs={{0,26},{2,24},{4,30},{6,28},{8,18},{10,16},{12,22},{14,20},{16,10}... | collective-permute-start | bytes 258056 | tf_op jit(solution)/shard_map/cond/branch_5_fun/ppermute | solution.py:297
  25.5 12.7 %collective-permute-start.80 = (bf16[336,128]{1,0:T(8,128)(2,1)S(1)}, bf16[336,128]{1,0:T(8,128)(2,1)S(1)}, u32[]{:S(2)}, u32[]{:S(2)}) collective-permute-start(bf16[336,128]{1,0:T(8,128)(2,1)S(1)} %get-tuple-element.250), channel_id=1, source_target_pairs={{0,10},{2,8},{4,14},{6,12},{8,2},{10,0},{12,6},{14,4},{16,26},{18,... | collective-permute-start | bytes 258056 | tf_op jit(solution)/shard_map/cond/branch_5_fun/ppermute | solution.py:297
  25.6 14.1 %collective-permute-start.81 = (bf16[336,128]{1,0:T(8,128)(2,1)S(1)}, bf16[336,128]{1,0:T(8,128)(2,1)S(1)}, u32[]{:S(2)}, u32[]{:S(2)}) collective-permute-start(bf16[336,128]{1,0:T(8,128)(2,1)S(1)} %get-tuple-element.251), channel_id=1, source_target_pairs={{0,24},{2,26},{4,28},{6,30},{8,16},{10,18},{12,20},{14,22},{16,8},... | collective-permute-start | bytes 258056 | tf_op jit(solution)/shard_map/cond/branch_5_fun/ppermute | solution.py:297
  29.4 13.1 %collective-permute-start.82 = (bf16[336,128]{1,0:T(8,128)(2,1)S(1)}, bf16[336,128]{1,0:T(8,128)(2,1)S(1)}, u32[]{:S(2)}, u32[]{:S(2)}) collective-permute-start(bf16[336,128]{1,0:T(8,128)(2,1)S(1)} %get-tuple-element.252.after_ref), channel_id=1, source_target_pairs={{0,8},{2,10},{4,12},{6,14},{8,0},{10,2},{12,4},{14,6},{16,24},{18,... | collective-permute-start | bytes 258056 | tf_op jit(solution)/shard_map/cond/branch_5_fun/ppermute | solution.py:297
  30.5 13.1 %collective-permute-start.83 = (bf16[336,128]{1,0:T(8,128)(2,1)S(1)}, bf16[336,128]{1,0:T(8,128)(2,1)S(1)}, u32[]{:S(2)}, u32[]{:S(2)}) collective-permute-start(bf16[336,128]{1,0:T(8,128)(2,1)S(1)} %get-tuple-element.253), channel_id=1, source_target_pairs={{0,22},{2,20},{4,18},{6,16},{8,30},{10,28},{12,26},{14,24},{16,6},... | collective-permute-start | bytes 258056 | tf_op jit(solution)/shard_map/cond/branch_5_fun/ppermute | solution.py:297
  34.3 9.8 %collective-permute-start.84 = (bf16[336,128]{1,0:T(8,128)(2,1)S(1)}, bf16[336,128]{1,0:T(8,128)(2,1)S(1)}, u32[]{:S(2)}, u32[]{:S(2)}) collective-permute-start(bf16[336,128]{1,0:T(8,128)(2,1)S(1)} %get-tuple-element.254), channel_id=1, source_target_pairs={{0,6},{2,4},{4,2},{6,0},{8,14},{10,12},{12,10},{14,8},{16,22},{18,... | collective-permute-start | bytes 258056 | tf_op jit(solution)/shard_map/cond/branch_5_fun/ppermute | solution.py:297
  38.2 10.1 %collective-permute-start.85 = (bf16[336,128]{1,0:T(8,128)(2,1)S(1)}, bf16[336,128]{1,0:T(8,128)(2,1)S(1)}, u32[]{:S(2)}, u32[]{:S(2)}) collective-permute-start(bf16[336,128]{1,0:T(8,128)(2,1)S(1)} %get-tuple-element.255), channel_id=1, source_target_pairs={{0,20},{2,22},{4,16},{6,18},{8,28},{10,30},{12,24},{14,26},{16,4},... | collective-permute-start | bytes 258056 | tf_op jit(solution)/shard_map/cond/branch_5_fun/ppermute | solution.py:297
  39.7 11.1 %collective-permute-start.87 = (bf16[336,128]{1,0:T(8,128)(2,1)S(1)}, bf16[336,128]{1,0:T(8,128)(2,1)S(1)}, u32[]{:S(2)}, u32[]{:S(2)}) collective-permute-start(bf16[336,128]{1,0:T(8,128)(2,1)S(1)} %get-tuple-element.257), channel_id=1, source_target_pairs={{0,18},{2,16},{4,22},{6,20},{8,26},{10,24},{12,30},{14,28},{16,2},... | collective-permute-start | bytes 258056 | tf_op jit(solution)/shard_map/cond/branch_5_fun/ppermute | solution.py:297
  42.5 8.3 %collective-permute-start.88 = (bf16[336,128]{1,0:T(8,128)(2,1)S(1)}, bf16[336,128]{1,0:T(8,128)(2,1)S(1)}, u32[]{:S(2)}, u32[]{:S(2)}) collective-permute-start(bf16[336,128]{1,0:T(8,128)(2,1)S(1)} %get-tuple-element.258), channel_id=1, source_target_pairs={{0,2},{2,0},{4,6},{6,4},{8,10},{10,8},{12,14},{14,12},{16,18},{18,... | collective-permute-start | bytes 258056 | tf_op jit(solution)/shard_map/cond/branch_5_fun/ppermute | solution.py:297
  43.6 8.0 %collective-permute-start.89 = (bf16[336,128]{1,0:T(8,128)(2,1)S(1)}, bf16[336,128]{1,0:T(8,128)(2,1)S(1)}, u32[]{:S(2)}, u32[]{:S(2)}) collective-permute-start(bf16[336,128]{1,0:T(8,128)(2,1)S(1)} %get-tuple-element.259), channel_id=1, source_target_pairs={{0,16},{2,18},{4,20},{6,22},{8,24},{10,26},{12,28},{14,30},{16,0},... | collective-permute-start | bytes 258056 | tf_op jit(solution)/shard_map/cond/branch_5_fun/ppermute | solution.py:297
  44.1 7.5 %collective-permute-start.86 = (bf16[336,128]{1,0:T(8,128)(2,1)S(1)}, bf16[336,128]{1,0:T(8,128)(2,1)S(1)}, u32[]{:S(2)}, u32[]{:S(2)}) collective-permute-start(bf16[336,128]{1,0:T(8,128)(2,1)S(1)} %get-tuple-element.256.after_ref), channel_id=1, source_target_pairs={{0,4},{2,6},{4,0},{6,2},{8,12},{10,14},{12,8},{14,10},{16,20},{18,... | collective-permute-start | bytes 258056 | tf_op jit(solution)/shard_map/cond/branch_5_fun/ppermute | solution.py:297
  55.7 0.6 %copy-start.4 = (f32[128,128]{1,0:T(8,128)}, f32[128,128]{1,0:T(8,128)S(1)}, u32[]{:S(2)}) copy-start(f32[128,128]{1,0:T(8,128)S(1)} %get-tuple-element.928) | copy-start | bytes 196612
